TPU v7x, 128 devices: a whole 4x4x4 slice. The times are simulated.
128 devices in a mesh: circ: 16 (over z_hi, y, core), axial: 8 (over z_lo, x).
Axes of the slice: x: 4, y: 4, z: 4 (z_hi: 2, z_lo: 2; z = z_hi * 2 + z_lo), core: 2. Of those that a mesh axis runs over, the one named last changes fastest.
Arguments:
- flow_state: float32 [5, 256, 16384], P(None, 'circ', 'axial'), may hold values from -6 to 6
- circ_speed: float32 [256, 16384], P('circ', 'axial'), may hold values from -1 to 1
- axial_speed: float32 [256, 16384], P('circ', 'axial'), may hold values from -1 to 1
- time_step: float32 [256, 16384], P('circ', 'axial'), may hold values from 0.05 to 0.25
- lsq_weights: float32 [256, 64, 192], P('axial'), may hold values from -0.4375 to 0.4375
- partner: int32 [16384], P('axial'), may hold values from 0 to 2047, as said below
- merge_owner: int32 [16384, 1], P(('circ', 'axial')), may hold values from 0 to 127, as said below
- merge_source: int32 [16384], P(('circ', 'axial')), may hold values from 0 to 511
- merge_host: int32 [16384], P(('circ', 'axial')), may hold values from 0 to 511
- merge_frac: float32 [16384, 64], P(('circ', 'axial')), may hold values from 0.3 to 1
Outputs:
- new_state: float32 [5, 256, 16384], P(None, 'circ', 'axial')
- last_rate: float32 [5, 256, 16384], P(None, 'circ', 'axial')
Inputs may be any that keep to these rules, and one draw needn't show every extreme that they name: `partner`: each aligned group of 2048 entries is a permutation of 0 to 2047; it names a column within the same group. `merge_owner`: owner g is the device at circ index g // 8 and axial index g % 8. The owner of a device's block is that device itself or a neighbour whose circ index differs by at most one (around the closed circ axis) and whose axial index differs by at most one. Among the 128 rows of one device no owner other than the device itself appears more than 8 times, and some other owner appears exactly 8 times. `merge_source`: A block number row * 32 + axial block on the sending device. `merge_host`: A block number row * 32 + axial block on the owning device.
All inputs are finite; a program needn't handle non-finite values.
Results may differ from a plain program's by a relative error of at most 0.0001.
Values sent between devices are 32-bit elements; how exact they have to be, the bound alone decides.
A program may use at most 128 MiB of HBM per device.

v0:
```python
import jax
import jax.numpy as jnp
from jax import lax
from jax.experimental import pallas as pl
from jax.experimental.pallas import tpu as pltpu
from jax.sharding import PartitionSpec as P

STEPS = 2
BALANCES = 2 * STEPS
CAP = 8
NV = 5
ROWS = 16
LANES = 128
TILES = 16
HALF = 64
SMALL = 128
BLOCKS = 32
N_CIRC = 16
N_AXIAL = 8
STACK = NV * ROWS
WIDE = NV * LANES
FIRST = 8
MESH = pl.DeviceIdType.MESH
F32 = jnp.float32
BF16 = jnp.bfloat16
NEIGHBOURS = [(dc, da) for dc in (-1, 0, 1) for da in (-1, 0, 1) if (dc, da) != (0, 0)]


def split(x):
    high = x.astype(BF16)
    return high, (x - high.astype(F32)).astype(BF16)


def lanes_of(shape):
    return lax.broadcasted_iota(jnp.int32, shape, len(shape) - 1)


def rolled(x, steps):
    return pltpu.roll(x, steps, x.ndim - 1)


def var_rows(v):
    return slice(v * ROWS, (v + 1) * ROWS)


def var_lanes(v):
    return slice(v * LANES, (v + 1) * LANES)


def cells(p):
    return pl.ds(pl.multiple_of(p * LANES, LANES), LANES)


def kernel(
    flow, cspd, aspd, dt, w, partner_row, partner_tile, owner, source, host, frac,
    out_u, out_rate,
    cur, base, cs, xs, wts, s32, shi, slo, rc, gout, gloc, fout, floc, a_loc, a_arr, c_loc, c_arr,
    edges, consts, f_keep, halo, perm, permuted,
    ax_send, ax_recv, ini_send, ini_recv, ci_send, ci_recv, lab_send, lab_recv, outbox, inbox,
    ax_ss, ax_rs, ini_ss, ini_rs, ci_ss, ci_rs, lab_ss, lab_rs, box_ss, box_rs,
):
    c = lax.axis_index("circ")
    a = lax.axis_index("axial")

    def peer(dc, da):
        return (lax.rem(c + dc + N_CIRC, N_CIRC), lax.rem(a + da + N_AXIAL, N_AXIAL))

    def remote(src, dst, send, recv, dc, da):
        return pltpu.make_async_remote_copy(
            src_ref=src, dst_ref=dst, send_sem=send, recv_sem=recv,
            device_id=peer(dc, da), device_id_type=MESH,
        )

    def axial_copy(n, side):
        return remote(
            ax_send.at[n, side], ax_recv.at[n, side], ax_ss.at[n, side], ax_rs.at[n, side],
            0, 2 * side - 1,
        )

    def init_copy(side):
        return remote(
            ini_send.at[side], ini_recv.at[side], ini_ss.at[side], ini_rs.at[side], 0, 2 * side - 1
        )

    def circ_copy(n, side):
        return remote(
            ci_send.at[n, side], ci_recv.at[n, side], ci_ss.at[n, side], ci_rs.at[n, side],
            2 * side - 1, 0,
        )

    def label_copy(k):
        dc, da = NEIGHBOURS[k]
        rows = pl.ds(k * CAP, CAP)
        return remote(lab_send.at[rows], lab_recv.at[rows], lab_ss.at[k], lab_rs.at[k], dc, da)

    def box_copy(n, k):
        dc, da = NEIGHBOURS[k]
        rows = pl.ds(k * CAP, CAP)
        return remote(
            outbox.at[n, rows], inbox.at[n, rows], box_ss.at[n, k], box_rs.at[n, k], dc, da
        )

    own = slice(FIRST, FIRST + ROWS)
    lane = lanes_of((ROWS, LANES))

    barrier = pltpu.get_barrier_semaphore()
    for dc, da in NEIGHBOURS:
        pl.semaphore_signal(barrier, inc=1, device_id=peer(dc, da), device_id_type=MESH)

    def stage(p, _):
        for v in range(NV):
            cur[p, v, own, :] = flow[v, :, cells(p)]
        cs[p, own, :] = cspd[:, cells(p)]
        return 0

    lax.fori_loop(0, TILES, stage, 0)

    for v in range(NV):
        ax_send[0, 0, var_rows(v), :] = jnp.where(lane < HALF, cur[0, v, own, :], 0.0)
        ax_send[0, 1, var_rows(v), :] = jnp.where(lane >= HALF, cur[TILES - 1, v, own, :], 0.0)
    ini_send[0, 0] = dt[:, 0:LANES]
    ini_send[0, 1] = dt[:, 0:LANES]
    ini_send[1, 0] = dt[:, (TILES - 1) * LANES:]
    ini_send[1, 1] = aspd[:, (TILES - 1) * LANES:]
    edges[...] = jnp.zeros_like(edges)

    square = (SMALL, SMALL)
    t_row = owner[...]
    s_row = source[...]
    h_row = host[...]

    def as_columns(row):
        return jnp.broadcast_to(row.astype(F32), square).T.astype(jnp.int32)

    t_col, s_col, h_col = as_columns(t_row), as_columns(s_row), as_columns(h_row)
    myself = c * N_AXIAL + a
    first = lax.broadcasted_iota(jnp.int32, square, 0)
    second = lax.broadcasted_iota(jnp.int32, square, 1)
    shares = jnp.where((jnp.broadcast_to(t_row, square) == t_col) & (first < second), 1.0, 0.0)
    rank = jnp.sum(shares, axis=0, keepdims=True).astype(jnp.int32)
    circ_off = ((t_row >> 3) - c + 1 + N_CIRC) & (N_CIRC - 1)
    number = circ_off * 3 + (t_row & (N_AXIAL - 1)) - a + 1
    number = jnp.where(number > 4, number - 1, number)
    place = jnp.where(t_row == myself, -1, number * CAP + rank)
    slots = len(NEIGHBOURS) * CAP
    chosen = jnp.where(
        jnp.broadcast_to(place, (slots, SMALL))
        == lax.broadcasted_iota(jnp.int32, (slots, SMALL), 0),
        1.0, 0.0,
    )

    def row_index(s):
        return ((s & (BLOCKS - 1)) >> 1) * ROWS + (s >> 5)

    host_index = row_index(h_row)
    labels = jnp.sum(chosen * (host_index + 1).astype(F32), axis=1, keepdims=True) - 1.0
    lab_send[...] = jnp.broadcast_to(labels, (slots, LANES))

    pl.semaphore_wait(barrier, len(NEIGHBOURS))
    for side in range(2):
        axial_copy(0, side).start()
        init_copy(side).start()
    for k in range(len(NEIGHBOURS)):
        label_copy(k).start()

    frac_twice = jnp.concatenate([frac[...], frac[...]], axis=1)
    placed = jnp.where((second >> 6) == (h_col & 1), frac_twice, 0.0)
    same_half = (s_col & 1) == (h_col & 1)
    straight = jnp.where(same_half, placed, 0.0)
    crossed = jnp.where(same_half, 0.0, placed)
    is_local = t_col == myself
    floc[0] = jnp.where(is_local, straight, 0.0)
    floc[1] = jnp.where(is_local, crossed, 0.0)
    fout[0] = jnp.dot(chosen, straight, precision=lax.Precision.HIGHEST)
    fout[1] = jnp.dot(chosen, crossed, precision=lax.Precision.HIGHEST)
    s_index = row_index(s_col)
    pick = jnp.concatenate(
        [
            jnp.where(s_index == second, 1.0, 0.0),
            jnp.where(s_index == second + LANES, 1.0, 0.0),
        ],
        axis=1,
    ).astype(BF16)
    gloc[...] = pick
    gout[...] = jnp.dot(chosen.astype(BF16), pick, preferred_element_type=F32).astype(BF16)
    tall = (TILES * ROWS, SMALL)
    tall_rows = lax.broadcasted_iota(jnp.int32, tall, 0)
    wanted = jnp.where(t_row == myself, host_index, -1)
    land = jnp.where(jnp.broadcast_to(wanted, tall) == tall_rows, 1.0, 0.0).astype(BF16)
    a_loc[...] = jnp.concatenate([land, land], axis=1)

    @pl.when(c == N_CIRC - 1)
    def _():
        perm[0] = partner_tile[...] >> 7
        perm[1] = partner_tile[...] & (LANES - 1)

    @pl.when(c == 0)
    def _():
        columns = TILES * LANES
        target = partner_row[...]
        upper = jnp.where(
            jnp.broadcast_to(target >> 7, (TILES, columns))
            == lax.broadcasted_iota(jnp.int32, (TILES, columns), 0),
            1.0, 0.0,
        ).astype(BF16)
        tall_lanes = (LANES, columns)
        here = jnp.broadcast_to(target & (LANES - 1), tall_lanes) == lax.broadcasted_iota(
            jnp.int32, tall_lanes, 0
        )
        position = lanes_of(tall_lanes)
        for part, value in enumerate((position >> 7, position & (LANES - 1))):
            lower = jnp.where(here, value.astype(F32), 0.0).astype(BF16)
            perm[part] = lax.dot_general(
                upper, lower, (((1,), (1,)), ((), ())), preferred_element_type=F32
            ).astype(jnp.int32)

    def weigh(p, _):
        gap = jnp.zeros((HALF, HALF), F32)
        both = jnp.concatenate(
            [
                jnp.concatenate([w[2 * p], gap], axis=1),
                jnp.concatenate([gap, w[2 * p + 1]], axis=1),
            ],
            axis=0,
        )
        high, low = split(both.T)
        wts[p, :, 0:LANES] = high
        wts[p, :, LANES:] = low
        return 0

    lax.fori_loop(0, TILES, weigh, 0)

    for k in range(len(NEIGHBOURS)):
        label_copy(k).wait()
    arrived_labels = lab_recv[...].astype(jnp.int32)
    label_row = (
        jnp.concatenate([arrived_labels, arrived_labels], axis=0).astype(F32).T.astype(jnp.int32)
    )
    a_arr[...] = jnp.where(
        jnp.concatenate([label_row, label_row], axis=0) == tall_rows, 1.0, 0.0
    ).astype(BF16)
    for side in range(2):
        init_copy(side).wait()
    consts[0] = jnp.where(a > 0, ini_recv[1, 0], 0.0)
    consts[1] = jnp.where(a < N_AXIAL - 1, ini_recv[0, 0], 0.0)
    consts[2] = jnp.where((a > 0) & (lane == 0), rolled(ini_recv[1, 1], 1), 0.0)
    consts[3] = jnp.where(lane == LANES - 1, aspd[:, (TILES - 1) * LANES:], 0.0)

    def fix_edges(n, factor, also_rate):
        for side in range(2):
            axial_copy(n, side).wait()
        left_speed, right_speed = consts[2], consts[3]
        last = (TILES - 1) * LANES
        for v in range(NV):
            vr = var_rows(v)
            from_left = jnp.where(a > 0, ax_recv[n, 1, vr, :], 0.0)
            from_right = jnp.where(a < N_AXIAL - 1, ax_recv[n, 0, vr, :], 0.0)
            left_flux = jnp.maximum(left_speed, 0.0) * from_left + jnp.minimum(
                left_speed, 0.0
            ) * edges[0, vr, :]
            right_flux = jnp.maximum(right_speed, 0.0) * edges[1, vr, :] + jnp.minimum(
                right_speed, 0.0
            ) * from_right
            cur[0, v, own, :] = cur[0, v, own, :] + factor * dt[:, 0:LANES] * left_flux
            cur[TILES - 1, v, own, :] = (
                cur[TILES - 1, v, own, :] - factor * dt[:, last:] * right_flux
            )
            if also_rate:
                out_rate[v, :, 0:LANES] = out_rate[v, :, 0:LANES] - left_flux
                out_rate[v, :, last:] = out_rate[v, :, last:] + right_flux
            else:
                halo[0, v] = from_left - factor * consts[0] * rolled(left_flux, LANES - 1)
                halo[1, v] = from_right + factor * consts[1] * rolled(right_flux, 1)

    def shift(q, left_tile, right_tile):
        for v in range(NV):
            moved = rolled(jnp.where(lane >= HALF, left_tile(v), right_tile(v)), HALF)
            high, low = split(moved)
            xs[q, var_rows(v), :] = high
            xs[q, STACK + v * ROWS:STACK + (v + 1) * ROWS, :] = low

    def slopes(p):
        left = jnp.concatenate([xs[p], xs[p + 1]], axis=1)
        full = jnp.dot(left, wts[p], preferred_element_type=F32)
        total = full[:STACK, :LANES] + full[:STACK, LANES:] + full[STACK:, :LANES]
        s32[p] = total
        high, low = split(total)
        rows = pl.ds(pl.multiple_of(p * ROWS, ROWS), ROWS)
        for v in range(NV):
            shi[rows, var_lanes(v)] = high[var_rows(v)]
            slo[rows, var_lanes(v)] = low[var_rows(v)]

    def gathered(picks, factors, v):
        vl = var_lanes(v)
        picked = jnp.dot(picks[...], shi[:, vl], preferred_element_type=F32) + jnp.dot(
            picks[...], slo[:, vl], preferred_element_type=F32
        )
        return picked * factors[0] + rolled(picked, HALF) * factors[1]

    def scatter(matrix, values, v):
        added = jnp.dot(matrix[...], values[:, var_lanes(v)], preferred_element_type=F32)
        for p in range(TILES):
            s32[p, var_rows(v), :] = s32[p, var_rows(v), :] + added[p * ROWS:(p + 1) * ROWS]

    def circ_pack(n):
        def pack(p, _):
            for v in range(NV):
                pair = slice(2 * v, 2 * v + 2)
                ci_send[n, 0, p, pair, :] = cur[p, v, FIRST:FIRST + 2, :]
                ci_send[n, 1, p, pair, :] = cur[p, v, FIRST + ROWS - 2:FIRST + ROWS, :]
            ci_send[n, 1, p, 10:11, :] = cs[p, FIRST + ROWS - 1:FIRST + ROWS, :]
            return 0

        lax.fori_loop(0, TILES, pack, 0)

    def unpack(upper, lower):
        def one(p, _):
            for v in range(NV):
                pair = slice(2 * v, 2 * v + 2)
                if upper is not None:
                    cur[p, v, FIRST + ROWS:FIRST + ROWS + 2, :] = upper[p, pair, :]
                if lower is not None:
                    cur[p, v, FIRST - 2:FIRST, :] = lower[p, pair, :]
            if lower is not None:
                cs[p, FIRST - 1:FIRST, :] = lower[p, 10:11, :]
            return 0

        lax.fori_loop(0, TILES, one, 0)

    def permute(rows):
        def one(p, _):
            tile = jnp.broadcast_to(perm[0, pl.ds(p, 1), :], (ROWS, LANES))
            column = jnp.broadcast_to(perm[1, pl.ds(p, 1), :], (ROWS, LANES))
            total = jnp.zeros((ROWS, LANES), F32)
            for q in range(TILES):
                found = jnp.take_along_axis(rows[q], column, axis=1)
                total = jnp.where(tile == q, found, total)
            permuted[p] = total
            return 0

        lax.fori_loop(0, TILES, one, 0)

    def circ_rates(p, _):
        above = cs[p, own, :]
        below = cs[p, FIRST - 1:FIRST + ROWS - 1, :]
        above_pos, above_neg = jnp.maximum(above, 0.0), jnp.minimum(above, 0.0)
        below_pos, below_neg = jnp.maximum(below, 0.0), jnp.minimum(below, 0.0)
        for v in range(NV):
            at = [cur[p, v, FIRST + k:FIRST + k + ROWS, :] for k in (-2, -1, 0, 1, 2)]
            slope_below = 0.25 * (at[2] - at[0])
            slope_here = 0.25 * (at[3] - at[1])
            slope_above = 0.25 * (at[4] - at[2])
            upper = above_pos * (at[2] + slope_here) + above_neg * (at[3] - slope_above)
            lower = below_pos * (at[1] + slope_below) + below_neg * (at[2] - slope_here)
            rc[p, var_rows(v), :] = upper - lower
        return 0

    def face(p, v, kind):
        half_slope = 0.5 * s32[p, var_rows(v), :]
        here = cur[p, v, own, :]
        return here + half_slope if kind == 0 else here - half_slope

    def flux(p, v, right_lane):
        speed = aspd[:, cells(p)]
        right = rolled(jnp.where(lane == 0, right_lane, face(p, v, 1)), LANES - 1)
        return jnp.maximum(speed, 0.0) * face(p, v, 0) + jnp.minimum(speed, 0.0) * right

    def advance(p, v, flux_here, flux_left, first_stage, factor):
        before = rolled(jnp.where(lane == LANES - 1, flux_left, flux_here), 1)
        rate = rc[p, var_rows(v), :] + flux_here - before
        here = cur[p, v, own, :]
        start = jnp.where(first_stage, here, base[p, var_rows(v), :])
        base[p, var_rows(v), :] = start
        out_rate[v, :, cells(p)] = rate
        new = 0.5 * (start + here) - factor * (dt[:, cells(p)] * rate)
        cur[p, v, own, :] = new
        return new

    def balance(n, _):
        odd = lax.rem(n, 2)
        first_stage = odd == 0
        factor = jnp.where(first_stage, 1.0, 0.5).astype(F32)
        earlier = jnp.where(first_stage, 0.5, 1.0).astype(F32)

        def shift_inner(q, _):
            shift(q, lambda v: cur[q - 1, v, own, :], lambda v: cur[q, v, own, :])
            return 0

        def slopes_inner(p, _):
            slopes(p)
            return 0

        lax.fori_loop(1, TILES, shift_inner, 0)
        lax.fori_loop(1, TILES - 1, slopes_inner, 0)
        fix_edges(n, earlier, False)
        shift(0, lambda v: halo[0, v], lambda v: cur[0, v, own, :])
        shift(TILES, lambda v: cur[TILES - 1, v, own, :], lambda v: halo[1, v])
        slopes(0)
        slopes(TILES - 1)

        circ_pack(n)
        for side in range(2):
            circ_copy(n, side).start()
        for v in range(NV):
            outbox[n, :, var_lanes(v)] = gathered(gout, fout, v)
        for k in range(len(NEIGHBOURS)):
            box_copy(n, k).start()

        for v in range(NV):
            high, low = split(gathered(gloc, floc, v))
            c_loc[:SMALL, var_lanes(v)] = high
            c_loc[SMALL:, var_lanes(v)] = low
        for v in range(NV):
            scatter(a_loc, c_loc, v)

        for side in range(2):
            circ_copy(n, side).wait()
        unpack(ci_recv.at[n, 0], ci_recv.at[n, 1])

        @pl.when(c == 0)
        def _():
            permute(ci_recv.at[n, 1])
            unpack(None, permuted)

        @pl.when(c == N_CIRC - 1)
        def _():
            permute(ci_recv.at[n, 0])
            unpack(permuted, None)

        lax.fori_loop(0, TILES, circ_rates, 0)

        for k in range(len(NEIGHBOURS)):
            box_copy(n, k).wait()
        for v in range(NV):
            high, low = split(inbox[n, :, var_lanes(v)])
            c_arr[:slots, var_lanes(v)] = high
            c_arr[slots:, var_lanes(v)] = low
        for v in range(NV):
            scatter(a_arr, c_arr, v)

        end = TILES - 1
        for v in range(NV):
            vr = var_rows(v)
            right_face = face(0, v, 1)
            flux_first = flux(0, v, face(1, v, 1))
            left_face = face(end, v, 0)
            flux_before = flux(end - 1, v, face(end, v, 1))
            flux_last = jnp.where(lane == LANES - 1, 0.0, flux(end, v, 0.0))
            edges[0, vr, :] = right_face
            edges[1, vr, :] = left_face
            f_keep[0, vr, :] = flux_first
            f_keep[1, vr, :] = flux_before
            new_first = advance(0, v, flux_first, 0.0, first_stage, factor)
            new_last = advance(end, v, flux_last, flux_before, first_stage, factor)
            ax_send[n + 1, 0, vr, :] = jnp.where(
                lane < HALF, new_first, rolled(right_face, LANES - 1)
            )
            ax_send[n + 1, 1, vr, :] = jnp.where(lane >= HALF, new_last, rolled(left_face, 1))
        for side in range(2):
            axial_copy(n + 1, side).start()

        def update(p, before):
            after = []
            for v in range(NV):
                here = flux(p, v, face(p + 1, v, 1))
                advance(p, v, here, before[v], first_stage, factor)
                after.append(here)
            return tuple(after)

        carried = tuple(f_keep[0, var_rows(v), :] for v in range(NV))
        carried = lax.fori_loop(1, end - 1, update, carried)
        for v in range(NV):
            advance(end - 1, v, f_keep[1, var_rows(v), :], carried[v], first_stage, factor)
        return 0

    lax.fori_loop(0, BALANCES, balance, 0)
    fix_edges(BALANCES, jnp.float32(0.5), True)

    def finish(p, _):
        for v in range(NV):
            out_u[v, :, cells(p)] = cur[p, v, own, :]
        return 0

    lax.fori_loop(0, TILES, finish, 0)


def local(
    flow_state, circ_speed, axial_speed, time_step, lsq_weights,
    partner, merge_owner, merge_source, merge_host, merge_frac,
):
    columns = TILES * LANES
    slots = len(NEIGHBOURS) * CAP
    vmem = pl.BlockSpec(memory_space=pltpu.VMEM)
    dma = pltpu.SemaphoreType.DMA
    shape = jax.ShapeDtypeStruct((NV, ROWS, columns), F32)
    scratch = [
        pltpu.VMEM((TILES, NV, 2 * ROWS, LANES), F32),
        pltpu.VMEM((TILES, STACK, LANES), F32),
        pltpu.VMEM((TILES, 2 * ROWS, LANES), F32),
        pltpu.VMEM((TILES + 1, 2 * STACK, LANES), BF16),
        pltpu.VMEM((TILES, 2 * LANES, 2 * LANES), BF16),
        pltpu.VMEM((TILES, STACK, LANES), F32),
        pltpu.VMEM((TILES * ROWS, WIDE), BF16),
        pltpu.VMEM((TILES * ROWS, WIDE), BF16),
        pltpu.VMEM((TILES, STACK, LANES), F32),
        pltpu.VMEM((slots, TILES * ROWS), BF16),
        pltpu.VMEM((SMALL, TILES * ROWS), BF16),
        pltpu.VMEM((2, slots, LANES), F32),
        pltpu.VMEM((2, SMALL, LANES), F32),
        pltpu.VMEM((TILES * ROWS, 2 * SMALL), BF16),
        pltpu.VMEM((TILES * ROWS, 2 * slots), BF16),
        pltpu.VMEM((2 * SMALL, WIDE), BF16),
        pltpu.VMEM((2 * slots, WIDE), BF16),
        pltpu.VMEM((2, STACK, LANES), F32),
        pltpu.VMEM((4, ROWS, LANES), F32),
        pltpu.VMEM((2, STACK, LANES), F32),
        pltpu.VMEM((2, NV, ROWS, LANES), F32),
        pltpu.VMEM((2, TILES, LANES), jnp.int32),
        pltpu.VMEM((TILES, ROWS, LANES), F32),
        pltpu.VMEM((BALANCES + 1, 2, STACK, LANES), F32),
        pltpu.VMEM((BALANCES + 1, 2, STACK, LANES), F32),
        pltpu.VMEM((2, 2, ROWS, LANES), F32),
        pltpu.VMEM((2, 2, ROWS, LANES), F32),
        pltpu.VMEM((BALANCES, 2, TILES, ROWS, LANES), F32),
        pltpu.VMEM((BALANCES, 2, TILES, ROWS, LANES), F32),
        pltpu.VMEM((slots, LANES), F32),
        pltpu.VMEM((slots, LANES), F32),
        pltpu.VMEM((BALANCES, slots, WIDE), F32),
        pltpu.VMEM((BALANCES, slots, WIDE), F32),
        dma((BALANCES + 1, 2)), dma((BALANCES + 1, 2)),
        dma((2,)), dma((2,)),
        dma((BALANCES, 2)), dma((BALANCES, 2)),
        dma((len(NEIGHBOURS),)), dma((len(NEIGHBOURS),)),
        dma((BALANCES, len(NEIGHBOURS))), dma((BALANCES, len(NEIGHBOURS))),
    ]
    return pl.pallas_call(
        kernel,
        out_shape=(shape, shape),
        in_specs=[vmem] * 11,
        out_specs=(vmem, vmem),
        scratch_shapes=scratch,
        compiler_params=pltpu.CompilerParams(
            collective_id=0, has_side_effects=True, vmem_limit_bytes=48 * 1024 * 1024
        ),
    )(
        flow_state, circ_speed, axial_speed, time_step, lsq_weights,
        partner.reshape(1, columns), partner.reshape(TILES, LANES),
        merge_owner.reshape(1, SMALL), merge_source.reshape(1, SMALL),
        merge_host.reshape(1, SMALL), merge_frac,
    )


def solution(mesh):
    in_specs = (
        P(None, "circ", "axial"),
        P("circ", "axial"),
        P("circ", "axial"),
        P("circ", "axial"),
        P("axial", None, None),
        P("axial"),
        P(("circ", "axial"), None),
        P(("circ", "axial")),
        P(("circ", "axial")),
        P(("circ", "axial"), None),
    )
    out_specs = (P(None, "circ", "axial"), P(None, "circ", "axial"))
    return jax.shard_map(local, mesh=mesh, in_specs=in_specs, out_specs=out_specs, check_vma=False)
```

profile of v0, /device:TPU:0, one launch (start us, length us, event | category | flops | bytes accessed | tf_op | source)
XLA Modules:
  0.0 86.9 jit_solution(2331761327582846575)
XLA Ops:
  0.6 0.8 copy.12.frac
  1.5 0.0 copy-start
  1.5 1.6 %copy-done = f32[32,64,192]{2,1,0:T(8,128)S(1)} copy-done((f32[32,64,192]{2,1,0:T(8,128)S(1)}, f32[32,64,192]{2,1,0:T(8,128)}, u32[]{:S(2)}) %copy-start) | copy-done | bytes 1572888
  3.1 0.0 copy-start.1
  3.1 1.1 %copy-done.1 = f32[5,16,2048]{2,1,0:T(8,128)S(1)} copy-done((f32[5,16,2048]{2,1,0:T(8,128)S(1)}, f32[5,16,2048]{2,1,0:T(8,128)}, u32[]{:S(2)}) %copy-start.1) | copy-done | bytes 655384
  4.2 0.0 copy-start.2
  4.2 0.9 %copy-done.2 = f32[16,2048]{1,0:T(8,128)S(1)} copy-done((f32[16,2048]{1,0:T(8,128)S(1)}, f32[16,2048]{1,0:T(8,128)}, u32[]{:S(2)}) %copy-start.2) | copy-done | bytes 131096
  5.1 0.0 copy-start.3
  5.1 0.9 %copy-done.3 = f32[16,2048]{1,0:T(8,128)S(1)} copy-done((f32[16,2048]{1,0:T(8,128)S(1)}, f32[16,2048]{1,0:T(8,128)}, u32[]{:S(2)}) %copy-start.3) | copy-done | bytes 131096
  6.0 0.0 copy-start.4
  6.0 0.9 %copy-done.4 = f32[16,2048]{1,0:T(8,128)S(1)} copy-done((f32[16,2048]{1,0:T(8,128)S(1)}, f32[16,2048]{1,0:T(8,128)}, u32[]{:S(2)}) %copy-start.4) | copy-done | bytes 131096
  6.9 0.0 copy-start.5
  6.9 0.7 copy-done.5
  7.6 0.0 copy-start.6
  7.6 0.7 copy-done.6
  8.2 0.0 copy-start.7
  8.2 0.7 copy-done.7
  8.9 0.0 copy-start.8
  8.9 0.7 copy-done.8
  9.5 75.7 %shard_map.113 = (f32[5,16,2048]{2,1,0:T(8,128)S(1)}, f32[5,16,2048]{2,1,0:T(8,128)S(1)}) custom-call(f32[5,16,2048]{2,1,0:T(8,128)S(1)} %copy-done.1, f32[16,2048]{1,0:T(8,128)S(1)} %copy-done.2, f32[16,2048]{1,0:T(8,128)S(1)} %copy-done.3, f32[16,2048]{1,0:T(8,128)S(1)} %copy-done.4, f32[32,64,192]{2,1,0:T(8,128)S(1)} %copy-done, s32[1,2048]{1,0:T(1,128)S(1)} %bitcast.5, ...), custom_call_target="tpu_custom_call" | custom-call | tf_op jit(solution)/shard_map/pallas_call | solution.py:536
  85.3 0.8 copy.15
  86.1 0.8 copy.16
Async XLA Ops:
  1.5 1.6 %copy-start = (f32[32,64,192]{2,1,0:T(8,128)S(1)}, f32[32,64,192]{2,1,0:T(8,128)}, u32[]{:S(2)}) copy-start(f32[32,64,192]{2,1,0:T(8,128)} %w.1) | copy-start | bytes 4718596
  3.1 1.1 %copy-start.1 = (f32[5,16,2048]{2,1,0:T(8,128)S(1)}, f32[5,16,2048]{2,1,0:T(8,128)}, u32[]{:S(2)}) copy-start(f32[5,16,2048]{2,1,0:T(8,128)} %flow.1) | copy-start | bytes 1966084
  4.2 0.9 %copy-start.2 = (f32[16,2048]{1,0:T(8,128)S(1)}, f32[16,2048]{1,0:T(8,128)}, u32[]{:S(2)}) copy-start(f32[16,2048]{1,0:T(8,128)} %cspd.1) | copy-start | bytes 393220
  5.1 0.9 %copy-start.3 = (f32[16,2048]{1,0:T(8,128)S(1)}, f32[16,2048]{1,0:T(8,128)}, u32[]{:S(2)}) copy-start(f32[16,2048]{1,0:T(8,128)} %aspd.1) | copy-start | bytes 393220
  6.0 0.9 %copy-start.4 = (f32[16,2048]{1,0:T(8,128)S(1)}, f32[16,2048]{1,0:T(8,128)}, u32[]{:S(2)}) copy-start(f32[16,2048]{1,0:T(8,128)} %dt.1) | copy-start | bytes 393220
  6.9 0.7 copy-start.5
  7.6 0.7 copy-start.6
  8.2 0.7 copy-start.7
  8.9 0.7 copy-start.8
where the time goes:
time: 87.3 us; the launch traced here: 86.9 us
  Pallas kernels  75.7 us (87%)
  local copies, waits for them, and re-layouts  10.6 us (12%)
    pallas_call x1, Pallas kernels, local(): pl.pallas_call(kernel, out_shape=(shape, shape), in_specs=[vmem] * 11, ou...  75.7 us
    unnamed x21, local copies, waits for them, and re-layouts  10.6 us

commit v1 on v0

--- a/solution.py
+++ b/solution.py
@@ -19,6 +19,8 @@
 N_AXIAL = 8
 STACK = NV * ROWS
 WIDE = NV * LANES
+ROW_TILES = 20
+EARLY = 17
 FIRST = 8
 MESH = pl.DeviceIdType.MESH
 F32 = jnp.float32
@@ -48,16 +50,18 @@
 
 
 def cells(p):
-    return pl.ds(pl.multiple_of(p * LANES, LANES), LANES)
+    return slice(p * LANES, (p + 1) * LANES)
 
 
 def kernel(
-    flow, cspd, aspd, dt, w, partner_row, partner_tile, owner, source, host, frac,
+    flow_hbm, cspd_hbm, aspd_hbm, dt_hbm, w_hbm, prow_hbm, ptile_hbm, owner_hbm, source_hbm,
+    host_hbm, frac_hbm,
     out_u, out_rate,
+    flow, cspd, aspd, dt, w, partner_row, partner_tile, owner, source, host, frac, load_sem,
     cur, base, cs, xs, wts, s32, shi, slo, rc, gout, gloc, fout, floc, a_loc, a_arr, c_loc, c_arr,
-    edges, consts, f_keep, halo, perm, permuted,
-    ax_send, ax_recv, ini_send, ini_recv, ci_send, ci_recv, lab_send, lab_recv, outbox, inbox,
-    ax_ss, ax_rs, ini_ss, ini_rs, ci_ss, ci_rs, lab_ss, lab_rs, box_ss, box_rs,
+    edges, consts, f_keep, halo, perm,
+    ax_send, ax_recv, ini_send, ini_recv, row_send, row_recv, ci_send, ci_recv, lab_send, lab_recv, outbox, inbox,
+    ax_ss, ax_rs, ini_ss, ini_rs, row_ss, row_rs, ci_ss, ci_rs, lab_ss, lab_rs, box_ss, box_rs,
 ):
     c = lax.axis_index("circ")
     a = lax.axis_index("axial")
@@ -82,11 +86,15 @@
             ini_send.at[side], ini_recv.at[side], ini_ss.at[side], ini_rs.at[side], 0, 2 * side - 1
         )
 
-    def circ_copy(n, side):
+    def circ_copy(n, side, late):
+        part = pl.ds(EARLY, ROW_TILES - EARLY) if late else pl.ds(0, EARLY)
         return remote(
-            ci_send.at[n, side], ci_recv.at[n, side], ci_ss.at[n, side], ci_rs.at[n, side],
-            2 * side - 1, 0,
-        )
+            ci_send.at[n, side, part], ci_recv.at[n, side, part],
+            ci_ss.at[n, side, late], ci_rs.at[n, side, late], 2 * side - 1, 0,
+        )
+
+    def row_copy():
+        return remote(row_send, row_recv, row_ss.at[0], row_rs.at[0], 1, 0)
 
     def label_copy(k):
         dc, da = NEIGHBOURS[k]
@@ -103,27 +111,43 @@
     own = slice(FIRST, FIRST + ROWS)
     lane = lanes_of((ROWS, LANES))
 
+    loads = [
+        pltpu.make_async_copy(src, dst, load_sem.at[i])
+        for i, (src, dst) in enumerate(
+            (
+                (owner_hbm, owner), (source_hbm, source), (host_hbm, host), (flow_hbm, flow),
+                (dt_hbm, dt), (aspd_hbm, aspd), (cspd_hbm, cspd), (frac_hbm, frac),
+                (prow_hbm, partner_row), (ptile_hbm, partner_tile), (w_hbm, w),
+            )
+        )
+    ]
+    for load in loads:
+        load.start()
+
     barrier = pltpu.get_barrier_semaphore()
     for dc, da in NEIGHBOURS:
         pl.semaphore_signal(barrier, inc=1, device_id=peer(dc, da), device_id_type=MESH)
 
-    def stage(p, _):
-        for v in range(NV):
-            cur[p, v, own, :] = flow[v, :, cells(p)]
-        cs[p, own, :] = cspd[:, cells(p)]
-        return 0
-
-    lax.fori_loop(0, TILES, stage, 0)
-
-    for v in range(NV):
-        ax_send[0, 0, var_rows(v), :] = jnp.where(lane < HALF, cur[0, v, own, :], 0.0)
-        ax_send[0, 1, var_rows(v), :] = jnp.where(lane >= HALF, cur[TILES - 1, v, own, :], 0.0)
-    ini_send[0, 0] = dt[:, 0:LANES]
-    ini_send[0, 1] = dt[:, 0:LANES]
-    ini_send[1, 0] = dt[:, (TILES - 1) * LANES:]
-    ini_send[1, 1] = aspd[:, (TILES - 1) * LANES:]
-    edges[...] = jnp.zeros_like(edges)
-
+    def pair_place(p, v):
+        slot = p - 1 if 0 < p < TILES - 1 else TILES - 2 + p // (TILES - 1)
+        if v < NV - 1:
+            return (slot if slot < TILES - 2 else slot + 3), 2 * v
+        group = slot // 4
+        return (TILES - 2 + group if group < 3 else ROW_TILES - 1), 2 * (slot % 4)
+
+    def pack_rows(n, p, v, tile):
+        where, row = pair_place(p, v)
+        ci_send[n, 0, where, row:row + 2, :] = tile[0:2]
+        ci_send[n, 1, where, row:row + 2, :] = tile[ROWS - 2:ROWS]
+
+    def shift(q, v, left_tile, right_tile):
+        moved = rolled(jnp.where(lane >= HALF, left_tile, right_tile), HALF)
+        high, low = split(moved)
+        xs[q, var_rows(v), :] = high
+        xs[q, STACK + v * ROWS:STACK + (v + 1) * ROWS, :] = low
+
+    for load in loads[:3]:
+        load.wait()
     square = (SMALL, SMALL)
     t_row = owner[...]
     s_row = source[...]
@@ -156,14 +180,45 @@
     labels = jnp.sum(chosen * (host_index + 1).astype(F32), axis=1, keepdims=True) - 1.0
     lab_send[...] = jnp.broadcast_to(labels, (slots, LANES))
 
+    for load in loads[3:7]:
+        load.wait()
+    for v in range(NV):
+        first_tile = flow[v, :, 0:LANES]
+        last_tile = flow[v, :, (TILES - 1) * LANES:]
+        ax_send[0, 0, var_rows(v), :] = jnp.where(lane < HALF, first_tile, 0.0)
+        ax_send[0, 1, var_rows(v), :] = jnp.where(lane >= HALF, last_tile, 0.0)
+    ini_send[0, 0] = dt[:, 0:LANES]
+    ini_send[0, 1] = dt[:, 0:LANES]
+    ini_send[1, 0] = dt[:, (TILES - 1) * LANES:]
+    ini_send[1, 1] = aspd[:, (TILES - 1) * LANES:]
+    edges[...] = jnp.zeros_like(edges)
     pl.semaphore_wait(barrier, len(NEIGHBOURS))
     for side in range(2):
         axial_copy(0, side).start()
         init_copy(side).start()
+    for p in range(TILES):
+        columns = slice(p * LANES, (p + 1) * LANES)
+        speed = cspd[:, columns]
+        cs[p, own, :] = speed
+        row_send[p:p + 1, :] = speed[ROWS - 1:ROWS]
+    row_copy().start()
+    for v in range(NV):
+        before = None
+        for p in range(TILES):
+            tile = flow[v, :, p * LANES:(p + 1) * LANES]
+            cur[p, v, own, :] = tile
+            pack_rows(0, p, v, tile)
+            if p > 0:
+                shift(p, v, before, tile)
+            before = tile
+    for side in range(2):
+        circ_copy(0, side, 0).start()
     for k in range(len(NEIGHBOURS)):
         label_copy(k).start()
 
-    frac_twice = jnp.concatenate([frac[...], frac[...]], axis=1)
+    for load in loads[7:10]:
+        load.wait()
+    frac_twice = jnp.concatenate([frac[...], frac[...]], axis=0).T
     placed = jnp.where((second >> 6) == (h_col & 1), frac_twice, 0.0)
     same_half = (s_col & 1) == (h_col & 1)
     straight = jnp.where(same_half, placed, 0.0)
@@ -189,7 +244,7 @@
     land = jnp.where(jnp.broadcast_to(wanted, tall) == tall_rows, 1.0, 0.0).astype(BF16)
     a_loc[...] = jnp.concatenate([land, land], axis=1)
 
-    @pl.when(c == N_CIRC - 1)
+    @pl.when(c > 0)
     def _():
         perm[0] = partner_tile[...] >> 7
         perm[1] = partner_tile[...] & (LANES - 1)
@@ -228,6 +283,7 @@
         wts[p, :, LANES:] = low
         return 0
 
+    loads[10].wait()
     lax.fori_loop(0, TILES, weigh, 0)
 
     for k in range(len(NEIGHBOURS)):
@@ -245,6 +301,20 @@
     consts[1] = jnp.where(a < N_AXIAL - 1, ini_recv[0, 0], 0.0)
     consts[2] = jnp.where((a > 0) & (lane == 0), rolled(ini_recv[1, 1], 1), 0.0)
     consts[3] = jnp.where(lane == LANES - 1, aspd[:, (TILES - 1) * LANES:], 0.0)
+
+    row_copy().wait()
+    for half in range(2):
+        some = slice(half * 8, half * 8 + 8)
+        below_row = row_recv[some, :]
+        mixed = jnp.zeros_like(below_row)
+        for q in range(TILES):
+            found = jnp.take_along_axis(
+                jnp.broadcast_to(row_recv[q:q + 1, :], below_row.shape), perm[1, some, :], axis=1
+            )
+            mixed = jnp.where(perm[0, some, :] == q, found, mixed)
+        below_row = jnp.where(c == 0, mixed, below_row)
+        for k in range(8):
+            cs[half * 8 + k, FIRST - 1:FIRST, :] = below_row[k:k + 1]
 
     def fix_edges(n, factor, also_rate):
         for side in range(2):
@@ -272,20 +342,13 @@
                 halo[0, v] = from_left - factor * consts[0] * rolled(left_flux, LANES - 1)
                 halo[1, v] = from_right + factor * consts[1] * rolled(right_flux, 1)
 
-    def shift(q, left_tile, right_tile):
-        for v in range(NV):
-            moved = rolled(jnp.where(lane >= HALF, left_tile(v), right_tile(v)), HALF)
-            high, low = split(moved)
-            xs[q, var_rows(v), :] = high
-            xs[q, STACK + v * ROWS:STACK + (v + 1) * ROWS, :] = low
-
     def slopes(p):
         left = jnp.concatenate([xs[p], xs[p + 1]], axis=1)
         full = jnp.dot(left, wts[p], preferred_element_type=F32)
         total = full[:STACK, :LANES] + full[:STACK, LANES:] + full[STACK:, :LANES]
         s32[p] = total
         high, low = split(total)
-        rows = pl.ds(pl.multiple_of(p * ROWS, ROWS), ROWS)
+        rows = slice(p * ROWS, (p + 1) * ROWS)
         for v in range(NV):
             shi[rows, var_lanes(v)] = high[var_rows(v)]
             slo[rows, var_lanes(v)] = low[var_rows(v)]
@@ -302,43 +365,52 @@
         for p in range(TILES):
             s32[p, var_rows(v), :] = s32[p, var_rows(v), :] + added[p * ROWS:(p + 1) * ROWS]
 
-    def circ_pack(n):
-        def pack(p, _):
+    def late_rows(n):
+        for v in range(NV):
+            for p in (0, TILES - 1):
+                pack_rows(n, p, v, cur[p, v, own, :])
+
+    def unpack(n, side):
+        start = FIRST - 2 if side else FIRST + ROWS
+        for p in range(TILES):
             for v in range(NV):
-                pair = slice(2 * v, 2 * v + 2)
-                ci_send[n, 0, p, pair, :] = cur[p, v, FIRST:FIRST + 2, :]
-                ci_send[n, 1, p, pair, :] = cur[p, v, FIRST + ROWS - 2:FIRST + ROWS, :]
-            ci_send[n, 1, p, 10:11, :] = cs[p, FIRST + ROWS - 1:FIRST + ROWS, :]
+                where, row = pair_place(p, v)
+                cur[p, v, start:start + 2, :] = ci_recv[n, side, where, row:row + 2, :]
+
+    def permute(n, side):
+        start = FIRST - 2 if side else FIRST + ROWS
+        rows = lax.broadcasted_iota(jnp.int32, (8, LANES), 0)
+        slot_of = [p - 1 if 0 < p < TILES - 1 else TILES - 2 + p // (TILES - 1) for p in range(TILES)]
+
+        def one(p):
+            tile = jnp.broadcast_to(perm[0, pl.ds(p, 1), :], (8, LANES))
+            column = jnp.broadcast_to(perm[1, pl.ds(p, 1), :], (8, LANES))
+            slot = jnp.where(
+                tile == 0, TILES - 2, jnp.where(tile == TILES - 1, TILES - 1, tile - 1)
+            )
+            total = jnp.zeros((8, LANES), F32)
+            for q in range(TILES):
+                where, _ = pair_place(q, 0)
+                found = jnp.take_along_axis(ci_recv[n, side, where], column, axis=1)
+                total = jnp.where(slot == slot_of[q], found, total)
+            last = jnp.zeros((8, LANES), F32)
+            offset = slot - (rows >> 1)
+            for g in range(4):
+                where = TILES - 2 + g if g < 3 else ROW_TILES - 1
+                found = jnp.take_along_axis(ci_recv[n, side, where], column, axis=1)
+                last = jnp.where(offset == 4 * g, found, last)
+            last = last + pltpu.roll(last, 4, 0)
+            last = last + pltpu.roll(last, 2, 0)
+            for v in range(NV - 1):
+                cur[p, v, start:start + 2, :] = total[2 * v:2 * v + 2]
+            cur[p, NV - 1, start:start + 2, :] = last[0:2]
+
+        def four(i, _):
+            for k in range(4):
+                one(4 * i + k)
             return 0
 
-        lax.fori_loop(0, TILES, pack, 0)
-
-    def unpack(upper, lower):
-        def one(p, _):
-            for v in range(NV):
-                pair = slice(2 * v, 2 * v + 2)
-                if upper is not None:
-                    cur[p, v, FIRST + ROWS:FIRST + ROWS + 2, :] = upper[p, pair, :]
-                if lower is not None:
-                    cur[p, v, FIRST - 2:FIRST, :] = lower[p, pair, :]
-            if lower is not None:
-                cs[p, FIRST - 1:FIRST, :] = lower[p, 10:11, :]
-            return 0
-
-        lax.fori_loop(0, TILES, one, 0)
-
-    def permute(rows):
-        def one(p, _):
-            tile = jnp.broadcast_to(perm[0, pl.ds(p, 1), :], (ROWS, LANES))
-            column = jnp.broadcast_to(perm[1, pl.ds(p, 1), :], (ROWS, LANES))
-            total = jnp.zeros((ROWS, LANES), F32)
-            for q in range(TILES):
-                found = jnp.take_along_axis(rows[q], column, axis=1)
-                total = jnp.where(tile == q, found, total)
-            permuted[p] = total
-            return 0
-
-        lax.fori_loop(0, TILES, one, 0)
+        lax.fori_loop(0, TILES // 4, four, 0)
 
     def circ_rates(p, _):
         above = cs[p, own, :]
@@ -381,26 +453,20 @@
         first_stage = odd == 0
         factor = jnp.where(first_stage, 1.0, 0.5).astype(F32)
         earlier = jnp.where(first_stage, 0.5, 1.0).astype(F32)
-
-        def shift_inner(q, _):
-            shift(q, lambda v: cur[q - 1, v, own, :], lambda v: cur[q, v, own, :])
-            return 0
-
-        def slopes_inner(p, _):
+        end = TILES - 1
+
+        for p in range(1, end):
             slopes(p)
-            return 0
-
-        lax.fori_loop(1, TILES, shift_inner, 0)
-        lax.fori_loop(1, TILES - 1, slopes_inner, 0)
         fix_edges(n, earlier, False)
-        shift(0, lambda v: halo[0, v], lambda v: cur[0, v, own, :])
-        shift(TILES, lambda v: cur[TILES - 1, v, own, :], lambda v: halo[1, v])
+        for v in range(NV):
+            shift(0, v, halo[0, v], cur[0, v, own, :])
+            shift(TILES, v, cur[end, v, own, :], halo[1, v])
+        late_rows(n)
+        for side in range(2):
+            circ_copy(n, side, 1).start()
         slopes(0)
-        slopes(TILES - 1)
-
-        circ_pack(n)
-        for side in range(2):
-            circ_copy(n, side).start()
+        slopes(end)
+
         for v in range(NV):
             outbox[n, :, var_lanes(v)] = gathered(gout, fout, v)
         for k in range(len(NEIGHBOURS)):
@@ -414,20 +480,27 @@
             scatter(a_loc, c_loc, v)
 
         for side in range(2):
-            circ_copy(n, side).wait()
-        unpack(ci_recv.at[n, 0], ci_recv.at[n, 1])
+            for late in range(2):
+                circ_copy(n, side, late).wait()
+
+        @pl.when(c > 0)
+        def _():
+            unpack(n, 1)
+
+        @pl.when(c < N_CIRC - 1)
+        def _():
+            unpack(n, 0)
 
         @pl.when(c == 0)
         def _():
-            permute(ci_recv.at[n, 1])
-            unpack(None, permuted)
+            permute(n, 1)
 
         @pl.when(c == N_CIRC - 1)
         def _():
-            permute(ci_recv.at[n, 0])
-            unpack(permuted, None)
-
-        lax.fori_loop(0, TILES, circ_rates, 0)
+            permute(n, 0)
+
+        for p in range(TILES):
+            circ_rates(p, 0)
 
         for k in range(len(NEIGHBOURS)):
             box_copy(n, k).wait()
@@ -438,7 +511,6 @@
         for v in range(NV):
             scatter(a_arr, c_arr, v)
 
-        end = TILES - 1
         for v in range(NV):
             vr = var_rows(v)
             right_face = face(0, v, 1)
@@ -459,29 +531,30 @@
         for side in range(2):
             axial_copy(n + 1, side).start()
 
-        def update(p, before):
-            after = []
-            for v in range(NV):
-                here = flux(p, v, face(p + 1, v, 1))
-                advance(p, v, here, before[v], first_stage, factor)
-                after.append(here)
-            return tuple(after)
-
-        carried = tuple(f_keep[0, var_rows(v), :] for v in range(NV))
-        carried = lax.fori_loop(1, end - 1, update, carried)
-        for v in range(NV):
-            advance(end - 1, v, f_keep[1, var_rows(v), :], carried[v], first_stage, factor)
+        for v in range(NV):
+            before = f_keep[0, var_rows(v), :]
+            tile = cur[0, v, own, :]
+            for p in range(1, end):
+                here = flux(p, v, face(p + 1, v, 1)) if p < end - 1 else f_keep[1, var_rows(v), :]
+                new = advance(p, v, here, before, first_stage, factor)
+                pack_rows(n + 1, p, v, new)
+                shift(p, v, tile, new)
+                before, tile = here, new
+            shift(end, v, tile, cur[end, v, own, :])
+
+        @pl.when(n < BALANCES - 1)
+        def _():
+            for side in range(2):
+                circ_copy(n + 1, side, 0).start()
+
         return 0
 
     lax.fori_loop(0, BALANCES, balance, 0)
     fix_edges(BALANCES, jnp.float32(0.5), True)
 
-    def finish(p, _):
+    for p in range(TILES):
         for v in range(NV):
             out_u[v, :, cells(p)] = cur[p, v, own, :]
-        return 0
-
-    lax.fori_loop(0, TILES, finish, 0)
 
 
 def local(
@@ -491,9 +564,22 @@
     columns = TILES * LANES
     slots = len(NEIGHBOURS) * CAP
     vmem = pl.BlockSpec(memory_space=pltpu.VMEM)
+    hbm = pl.BlockSpec(memory_space=pltpu.HBM)
     dma = pltpu.SemaphoreType.DMA
     shape = jax.ShapeDtypeStruct((NV, ROWS, columns), F32)
     scratch = [
+        pltpu.VMEM((NV, ROWS, columns), F32),
+        pltpu.VMEM((ROWS, columns), F32),
+        pltpu.VMEM((ROWS, columns), F32),
+        pltpu.VMEM((ROWS, columns), F32),
+        pltpu.VMEM((BLOCKS, HALF, 3 * HALF), F32),
+        pltpu.VMEM((1, columns), jnp.int32),
+        pltpu.VMEM((TILES, LANES), jnp.int32),
+        pltpu.VMEM((1, SMALL), jnp.int32),
+        pltpu.VMEM((1, SMALL), jnp.int32),
+        pltpu.VMEM((1, SMALL), jnp.int32),
+        pltpu.VMEM((HALF, SMALL), F32),
+        dma((11,)),
         pltpu.VMEM((TILES, NV, 2 * ROWS, LANES), F32),
         pltpu.VMEM((TILES, STACK, LANES), F32),
         pltpu.VMEM((TILES, 2 * ROWS, LANES), F32),
@@ -516,37 +602,39 @@
         pltpu.VMEM((2, STACK, LANES), F32),
         pltpu.VMEM((2, NV, ROWS, LANES), F32),
         pltpu.VMEM((2, TILES, LANES), jnp.int32),
-        pltpu.VMEM((TILES, ROWS, LANES), F32),
         pltpu.VMEM((BALANCES + 1, 2, STACK, LANES), F32),
         pltpu.VMEM((BALANCES + 1, 2, STACK, LANES), F32),
         pltpu.VMEM((2, 2, ROWS, LANES), F32),
         pltpu.VMEM((2, 2, ROWS, LANES), F32),
-        pltpu.VMEM((BALANCES, 2, TILES, ROWS, LANES), F32),
-        pltpu.VMEM((BALANCES, 2, TILES, ROWS, LANES), F32),
+        pltpu.VMEM((TILES, LANES), F32),
+        pltpu.VMEM((TILES, LANES), F32),
+        pltpu.VMEM((BALANCES + 1, 2, ROW_TILES, 8, LANES), F32),
+        pltpu.VMEM((BALANCES, 2, ROW_TILES, 8, LANES), F32),
         pltpu.VMEM((slots, LANES), F32),
         pltpu.VMEM((slots, LANES), F32),
         pltpu.VMEM((BALANCES, slots, WIDE), F32),
         pltpu.VMEM((BALANCES, slots, WIDE), F32),
         dma((BALANCES + 1, 2)), dma((BALANCES + 1, 2)),
         dma((2,)), dma((2,)),
-        dma((BALANCES, 2)), dma((BALANCES, 2)),
+        dma((1,)), dma((1,)),
+        dma((BALANCES, 2, 2)), dma((BALANCES, 2, 2)),
         dma((len(NEIGHBOURS),)), dma((len(NEIGHBOURS),)),
         dma((BALANCES, len(NEIGHBOURS))), dma((BALANCES, len(NEIGHBOURS))),
     ]
     return pl.pallas_call(
         kernel,
         out_shape=(shape, shape),
-        in_specs=[vmem] * 11,
+        in_specs=[hbm] * 11,
         out_specs=(vmem, vmem),
         scratch_shapes=scratch,
         compiler_params=pltpu.CompilerParams(
-            collective_id=0, has_side_effects=True, vmem_limit_bytes=48 * 1024 * 1024
+            collective_id=0, has_side_effects=True, vmem_limit_bytes=56 * 1024 * 1024
         ),
     )(
         flow_state, circ_speed, axial_speed, time_step, lsq_weights,
         partner.reshape(1, columns), partner.reshape(TILES, LANES),
         merge_owner.reshape(1, SMALL), merge_source.reshape(1, SMALL),
-        merge_host.reshape(1, SMALL), merge_frac,
+        merge_host.reshape(1, SMALL), merge_frac.T,
     )
 
 

time: 87.3 us -> 61.6 us (0.71)
  Pallas kernels: 75.7 us -> 56.9 us
  local copies, waits for them, and re-layouts: 10.6 us -> 3.95 us
    pallas_call x1, Pallas kernels: 75.7 us -> 56.9 us  [local(): pl.pallas_call(kernel, out_shape=(shape, shape), in_specs=[hbm] * 11, out...]
    unnamed x21 -> x2, local copies, waits for them, and re-layouts: 10.6 us -> 3.95 us
where the time goes in v1:
time: 61.6 us; the launch traced here: 61.4 us
  Pallas kernels  56.9 us (92%)
  local copies, waits for them, and re-layouts  3.95 us (6%)
  between operations  0.64 us (1%)
    pallas_call x1, Pallas kernels, local(): pl.pallas_call(kernel, out_shape=(shape, shape), in_specs=[hbm] * 11, out...  56.9 us
    unnamed x2, local copies, waits for them, and re-layouts  3.95 us

profile of v1, /device:TPU:0, one launch (start us, length us, event | category | flops | bytes accessed | tf_op | source)
XLA Modules:
  0.0 61.4 jit_solution(2796447382516272229)
XLA Ops:
  0.6 56.9 %shard_map.113 = (f32[5,16,2048]{2,1,0:T(8,128)}, f32[5,16,2048]{2,1,0:T(8,128)}) custom-call(f32[5,16,2048]{2,1,0:T(8,128)} %flow_hbm.1, f32[16,2048]{1,0:T(8,128)} %cspd_hbm.1, f32[16,2048]{1,0:T(8,128)} %aspd_hbm.1, f32[16,2048]{1,0:T(8,128)} %dt_hbm.1, f32[32,64,192]{2,1,0:T(8,128)} %w_hbm.1, s32[1,2048]{1,0:T(1,128)} %bitcast.7, s32[16,128]{1,0:T(8,128)} %bitcast.8, ...), custom_call_target="tpu_custom_call" | custom-call | tf_op jit(solution)/shard_map/pallas_call | solution.py:624
  57.5 2.0 %copy.14 = f32[5,16,2048]{2,1,0:T(8,128)} copy(f32[5,16,2048]{2,1,0:T(8,128)} %get-tuple-element.4) | data formatting | bytes 1310720
  59.5 2.0 %copy.15 = f32[5,16,2048]{2,1,0:T(8,128)} copy(f32[5,16,2048]{2,1,0:T(8,128)} %get-tuple-element.5) | data formatting | bytes 1310720

commit v2 on v1

--- a/solution.py
+++ b/solution.py
@@ -26,6 +26,8 @@
 F32 = jnp.float32
 BF16 = jnp.bfloat16
 NEIGHBOURS = [(dc, da) for dc in (-1, 0, 1) for da in (-1, 0, 1) if (dc, da) != (0, 0)]
+DIRECT = [(-1, 0), (1, 0), (0, -1), (0, 1)]
+FAR_FIRST = (0, 2, 5, 7, 1, 6, 3, 4)
 
 
 def split(x):
@@ -58,9 +60,9 @@
     host_hbm, frac_hbm,
     out_u, out_rate,
     flow, cspd, aspd, dt, w, partner_row, partner_tile, owner, source, host, frac, load_sem,
-    cur, base, cs, xs, wts, s32, shi, slo, rc, gout, gloc, fout, floc, a_loc, a_arr, c_loc, c_arr,
+    cur, base, cs, xs, wts, s32, shi, slo, rc, gout, gend, ends, gloc, fout, floc, a_loc, a_arr, a_edge, c_loc, c_arr,
     edges, consts, f_keep, halo, perm,
-    ax_send, ax_recv, ini_send, ini_recv, row_send, row_recv, ci_send, ci_recv, lab_send, lab_recv, outbox, inbox,
+    ax_send, ax_recv, ini_recv, row_send, row_recv, ci_send, ci_recv, lab_send, lab_recv, outbox, inbox, early_box,
     ax_ss, ax_rs, ini_ss, ini_rs, row_ss, row_rs, ci_ss, ci_rs, lab_ss, lab_rs, box_ss, box_rs,
 ):
     c = lax.axis_index("circ")
@@ -81,9 +83,18 @@
             0, 2 * side - 1,
         )
 
-    def init_copy(side):
+    head, tail = pl.ds(0, LANES), pl.ds((TILES - 1) * LANES, LANES)
+
+    def first_axial_copy(side):
         return remote(
-            ini_send.at[side], ini_recv.at[side], ini_ss.at[side], ini_rs.at[side], 0, 2 * side - 1
+            flow_hbm.at[:, :, tail if side else head], ax_recv.at[0, side],
+            ax_ss.at[0, side], ax_rs.at[0, side], 0, 2 * side - 1,
+        )
+
+    def init_copy(k):
+        source_of = (dt_hbm.at[:, head], dt_hbm.at[:, tail], aspd_hbm.at[:, tail])
+        return remote(
+            source_of[k], ini_recv.at[k], ini_ss.at[k], ini_rs.at[k], 0, 1 if k else -1
         )
 
     def circ_copy(n, side, late):
@@ -125,7 +136,7 @@
         load.start()
 
     barrier = pltpu.get_barrier_semaphore()
-    for dc, da in NEIGHBOURS:
+    for dc, da in DIRECT:
         pl.semaphore_signal(barrier, inc=1, device_id=peer(dc, da), device_id_type=MESH)
 
     def pair_place(p, v):
@@ -180,22 +191,15 @@
     labels = jnp.sum(chosen * (host_index + 1).astype(F32), axis=1, keepdims=True) - 1.0
     lab_send[...] = jnp.broadcast_to(labels, (slots, LANES))
 
+    edges[...] = jnp.zeros_like(edges)
+    consts[...] = jnp.zeros_like(consts)
+    pl.semaphore_wait(barrier, len(DIRECT))
+    for side in range(2):
+        first_axial_copy(side).start()
+    for k in range(3):
+        init_copy(k).start()
     for load in loads[3:7]:
         load.wait()
-    for v in range(NV):
-        first_tile = flow[v, :, 0:LANES]
-        last_tile = flow[v, :, (TILES - 1) * LANES:]
-        ax_send[0, 0, var_rows(v), :] = jnp.where(lane < HALF, first_tile, 0.0)
-        ax_send[0, 1, var_rows(v), :] = jnp.where(lane >= HALF, last_tile, 0.0)
-    ini_send[0, 0] = dt[:, 0:LANES]
-    ini_send[0, 1] = dt[:, 0:LANES]
-    ini_send[1, 0] = dt[:, (TILES - 1) * LANES:]
-    ini_send[1, 1] = aspd[:, (TILES - 1) * LANES:]
-    edges[...] = jnp.zeros_like(edges)
-    pl.semaphore_wait(barrier, len(NEIGHBOURS))
-    for side in range(2):
-        axial_copy(0, side).start()
-        init_copy(side).start()
     for p in range(TILES):
         columns = slice(p * LANES, (p + 1) * LANES)
         speed = cspd[:, columns]
@@ -213,9 +217,6 @@
             before = tile
     for side in range(2):
         circ_copy(0, side, 0).start()
-    for k in range(len(NEIGHBOURS)):
-        label_copy(k).start()
-
     for load in loads[7:10]:
         load.wait()
     frac_twice = jnp.concatenate([frac[...], frac[...]], axis=0).T
@@ -237,7 +238,10 @@
         axis=1,
     ).astype(BF16)
     gloc[...] = pick
-    gout[...] = jnp.dot(chosen.astype(BF16), pick, preferred_element_type=F32).astype(BF16)
+    picked_out = jnp.dot(chosen.astype(BF16), pick, preferred_element_type=F32)
+    gout[...] = picked_out.astype(BF16)
+    picked_end = jnp.concatenate([picked_out[:, :ROWS], picked_out[:, -ROWS:]], axis=1)
+    gend[...] = jnp.concatenate([picked_end, picked_end], axis=1).astype(BF16)
     tall = (TILES * ROWS, SMALL)
     tall_rows = lax.broadcasted_iota(jnp.int32, tall, 0)
     wanted = jnp.where(t_row == myself, host_index, -1)
@@ -286,35 +290,38 @@
     loads[10].wait()
     lax.fori_loop(0, TILES, weigh, 0)
 
-    for k in range(len(NEIGHBOURS)):
-        label_copy(k).wait()
-    arrived_labels = lab_recv[...].astype(jnp.int32)
-    label_row = (
-        jnp.concatenate([arrived_labels, arrived_labels], axis=0).astype(F32).T.astype(jnp.int32)
-    )
-    a_arr[...] = jnp.where(
-        jnp.concatenate([label_row, label_row], axis=0) == tall_rows, 1.0, 0.0
-    ).astype(BF16)
-    for side in range(2):
-        init_copy(side).wait()
-    consts[0] = jnp.where(a > 0, ini_recv[1, 0], 0.0)
-    consts[1] = jnp.where(a < N_AXIAL - 1, ini_recv[0, 0], 0.0)
-    consts[2] = jnp.where((a > 0) & (lane == 0), rolled(ini_recv[1, 1], 1), 0.0)
-    consts[3] = jnp.where(lane == LANES - 1, aspd[:, (TILES - 1) * LANES:], 0.0)
-
-    row_copy().wait()
-    for half in range(2):
-        some = slice(half * 8, half * 8 + 8)
-        below_row = row_recv[some, :]
-        mixed = jnp.zeros_like(below_row)
-        for q in range(TILES):
-            found = jnp.take_along_axis(
-                jnp.broadcast_to(row_recv[q:q + 1, :], below_row.shape), perm[1, some, :], axis=1
-            )
-            mixed = jnp.where(perm[0, some, :] == q, found, mixed)
-        below_row = jnp.where(c == 0, mixed, below_row)
-        for k in range(8):
-            cs[half * 8 + k, FIRST - 1:FIRST, :] = below_row[k:k + 1]
+    def receive_constants():
+        for k in range(3):
+            init_copy(k).wait()
+        consts[0] = jnp.where(a > 0, ini_recv[1], 0.0)
+        consts[1] = jnp.where(a < N_AXIAL - 1, ini_recv[0], 0.0)
+        consts[2] = jnp.where((a > 0) & (lane == 0), rolled(ini_recv[2], 1), 0.0)
+        consts[3] = jnp.where(lane == LANES - 1, aspd[:, (TILES - 1) * LANES:], 0.0)
+        row_copy().wait()
+        for half in range(2):
+            some = slice(half * 8, half * 8 + 8)
+            below_row = row_recv[some, :]
+            mixed = jnp.zeros_like(below_row)
+            for q in range(TILES):
+                found = jnp.take_along_axis(
+                    jnp.broadcast_to(row_recv[q:q + 1, :], below_row.shape), perm[1, some, :], axis=1
+                )
+                mixed = jnp.where(perm[0, some, :] == q, found, mixed)
+            below_row = jnp.where(c == 0, mixed, below_row)
+            for k in range(8):
+                cs[half * 8 + k, FIRST - 1:FIRST, :] = below_row[k:k + 1]
+
+    def receive_labels():
+        for k in range(len(NEIGHBOURS)):
+            label_copy(k).wait()
+        arrived = lab_recv[...]
+        label_row = jnp.concatenate([arrived, arrived], axis=0).T.astype(jnp.int32)
+        land_here = jnp.where(
+            jnp.concatenate([label_row, label_row], axis=0) == tall_rows, 1.0, 0.0
+        ).astype(BF16)
+        a_arr[...] = land_here[2 * ROWS:-2 * ROWS]
+        a_edge[0:2 * ROWS, :] = land_here[0:2 * ROWS]
+        a_edge[2 * ROWS:, :] = land_here[-2 * ROWS:]
 
     def fix_edges(n, factor, also_rate):
         for side in range(2):
@@ -323,8 +330,8 @@
         last = (TILES - 1) * LANES
         for v in range(NV):
             vr = var_rows(v)
-            from_left = jnp.where(a > 0, ax_recv[n, 1, vr, :], 0.0)
-            from_right = jnp.where(a < N_AXIAL - 1, ax_recv[n, 0, vr, :], 0.0)
+            from_left = jnp.where(a > 0, ax_recv[n, 1, v], 0.0)
+            from_right = jnp.where(a < N_AXIAL - 1, ax_recv[n, 0, v], 0.0)
             left_flux = jnp.maximum(left_speed, 0.0) * from_left + jnp.minimum(
                 left_speed, 0.0
             ) * edges[0, vr, :]
@@ -352,6 +359,10 @@
         for v in range(NV):
             shi[rows, var_lanes(v)] = high[var_rows(v)]
             slo[rows, var_lanes(v)] = low[var_rows(v)]
+            if p in (0, TILES - 1):
+                start = ROWS * (p // (TILES - 1))
+                ends[start:start + ROWS, var_lanes(v)] = high[var_rows(v)]
+                ends[2 * ROWS + start:3 * ROWS + start, var_lanes(v)] = low[var_rows(v)]
 
     def gathered(picks, factors, v):
         vl = var_lanes(v)
@@ -360,10 +371,10 @@
         )
         return picked * factors[0] + rolled(picked, HALF) * factors[1]
 
-    def scatter(matrix, values, v):
+    def scatter(matrix, values, v, tiles):
         added = jnp.dot(matrix[...], values[:, var_lanes(v)], preferred_element_type=F32)
-        for p in range(TILES):
-            s32[p, var_rows(v), :] = s32[p, var_rows(v), :] + added[p * ROWS:(p + 1) * ROWS]
+        for i, p in enumerate(tiles):
+            s32[p, var_rows(v), :] = s32[p, var_rows(v), :] + added[i * ROWS:(i + 1) * ROWS]
 
     def late_rows(n):
         for v in range(NV):
@@ -457,27 +468,44 @@
 
         for p in range(1, end):
             slopes(p)
+        for rows in (slice(0, ROWS), slice(end * ROWS, TILES * ROWS)):
+            shi[rows, :] = jnp.zeros((ROWS, WIDE), BF16)
+            slo[rows, :] = jnp.zeros((ROWS, WIDE), BF16)
+        for v in range(NV):
+            early_box[:, var_lanes(v)] = gathered(gout, fout, v)
         fix_edges(n, earlier, False)
         for v in range(NV):
             shift(0, v, halo[0, v], cur[0, v, own, :])
             shift(TILES, v, cur[end, v, own, :], halo[1, v])
+        slopes(0)
+        slopes(end)
+        for v in range(NV):
+            picked = jnp.dot(gend[...], ends[:, var_lanes(v)], preferred_element_type=F32)
+            outbox[n, :, var_lanes(v)] = (
+                early_box[:, var_lanes(v)] + picked * fout[0] + rolled(picked, HALF) * fout[1]
+            )
+        for k in FAR_FIRST:
+            box_copy(n, k).start()
+
+        @pl.when(n == 0)
+        def _():
+            for k in FAR_FIRST:
+                label_copy(k).start()
+
         late_rows(n)
         for side in range(2):
             circ_copy(n, side, 1).start()
-        slopes(0)
-        slopes(end)
-
-        for v in range(NV):
-            outbox[n, :, var_lanes(v)] = gathered(gout, fout, v)
-        for k in range(len(NEIGHBOURS)):
-            box_copy(n, k).start()
+
+        @pl.when(n == 0)
+        def _():
+            receive_constants()
 
         for v in range(NV):
             high, low = split(gathered(gloc, floc, v))
             c_loc[:SMALL, var_lanes(v)] = high
             c_loc[SMALL:, var_lanes(v)] = low
         for v in range(NV):
-            scatter(a_loc, c_loc, v)
+            scatter(a_loc, c_loc, v, range(TILES))
 
         for side in range(2):
             for late in range(2):
@@ -504,12 +532,17 @@
 
         for k in range(len(NEIGHBOURS)):
             box_copy(n, k).wait()
+
+        @pl.when(n == 0)
+        def _():
+            receive_labels()
+
         for v in range(NV):
             high, low = split(inbox[n, :, var_lanes(v)])
             c_arr[:slots, var_lanes(v)] = high
             c_arr[slots:, var_lanes(v)] = low
         for v in range(NV):
-            scatter(a_arr, c_arr, v)
+            scatter(a_edge, c_arr, v, (0, 1, end - 1, end))
 
         for v in range(NV):
             vr = var_rows(v)
@@ -524,13 +557,15 @@
             f_keep[1, vr, :] = flux_before
             new_first = advance(0, v, flux_first, 0.0, first_stage, factor)
             new_last = advance(end, v, flux_last, flux_before, first_stage, factor)
-            ax_send[n + 1, 0, vr, :] = jnp.where(
+            ax_send[n + 1, 0, v] = jnp.where(
                 lane < HALF, new_first, rolled(right_face, LANES - 1)
             )
-            ax_send[n + 1, 1, vr, :] = jnp.where(lane >= HALF, new_last, rolled(left_face, 1))
+            ax_send[n + 1, 1, v] = jnp.where(lane >= HALF, new_last, rolled(left_face, 1))
         for side in range(2):
             axial_copy(n + 1, side).start()
 
+        for v in range(NV):
+            scatter(a_arr, c_arr, v, range(2, end - 1))
         for v in range(NV):
             before = f_keep[0, var_rows(v), :]
             tile = cur[0, v, own, :]
@@ -590,11 +625,14 @@
         pltpu.VMEM((TILES * ROWS, WIDE), BF16),
         pltpu.VMEM((TILES, STACK, LANES), F32),
         pltpu.VMEM((slots, TILES * ROWS), BF16),
+        pltpu.VMEM((slots, 4 * ROWS), BF16),
+        pltpu.VMEM((4 * ROWS, WIDE), BF16),
         pltpu.VMEM((SMALL, TILES * ROWS), BF16),
         pltpu.VMEM((2, slots, LANES), F32),
         pltpu.VMEM((2, SMALL, LANES), F32),
         pltpu.VMEM((TILES * ROWS, 2 * SMALL), BF16),
-        pltpu.VMEM((TILES * ROWS, 2 * slots), BF16),
+        pltpu.VMEM(((TILES - 4) * ROWS, 2 * slots), BF16),
+        pltpu.VMEM((4 * ROWS, 2 * slots), BF16),
         pltpu.VMEM((2 * SMALL, WIDE), BF16),
         pltpu.VMEM((2 * slots, WIDE), BF16),
         pltpu.VMEM((2, STACK, LANES), F32),
@@ -602,10 +640,9 @@
         pltpu.VMEM((2, STACK, LANES), F32),
         pltpu.VMEM((2, NV, ROWS, LANES), F32),
         pltpu.VMEM((2, TILES, LANES), jnp.int32),
-        pltpu.VMEM((BALANCES + 1, 2, STACK, LANES), F32),
-        pltpu.VMEM((BALANCES + 1, 2, STACK, LANES), F32),
-        pltpu.VMEM((2, 2, ROWS, LANES), F32),
-        pltpu.VMEM((2, 2, ROWS, LANES), F32),
+        pltpu.VMEM((BALANCES + 1, 2, NV, ROWS, LANES), F32),
+        pltpu.VMEM((BALANCES + 1, 2, NV, ROWS, LANES), F32),
+        pltpu.VMEM((3, ROWS, LANES), F32),
         pltpu.VMEM((TILES, LANES), F32),
         pltpu.VMEM((TILES, LANES), F32),
         pltpu.VMEM((BALANCES + 1, 2, ROW_TILES, 8, LANES), F32),
@@ -614,8 +651,9 @@
         pltpu.VMEM((slots, LANES), F32),
         pltpu.VMEM((BALANCES, slots, WIDE), F32),
         pltpu.VMEM((BALANCES, slots, WIDE), F32),
+        pltpu.VMEM((slots, WIDE), F32),
         dma((BALANCES + 1, 2)), dma((BALANCES + 1, 2)),
-        dma((2,)), dma((2,)),
+        dma((3,)), dma((3,)),
         dma((1,)), dma((1,)),
         dma((BALANCES, 2, 2)), dma((BALANCES, 2, 2)),
         dma((len(NEIGHBOURS),)), dma((len(NEIGHBOURS),)),
@@ -623,7 +661,7 @@
     ]
     return pl.pallas_call(
         kernel,
-        out_shape=(shape, shape),
+        out_shape=(pltpu.VMEM((NV, ROWS, columns), F32),) * 2,
         in_specs=[hbm] * 11,
         out_specs=(vmem, vmem),
         scratch_shapes=scratch,

time: 61.6 us -> 56.6 us (0.919)
  Pallas kernels: 56.9 us -> 54.2 us
  local copies, waits for them, and re-layouts: 3.95 us -> 1.67 us
    pallas_call x1, Pallas kernels: 56.9 us -> 54.2 us  [local(): pl.pallas_call(kernel, out_shape=(pltpu.VMEM((NV, ROWS, columns), F32),)...]
    unnamed x2, local copies, waits for them, and re-layouts: 3.95 us -> 1.67 us
where the time goes in v2:
time: 56.6 us; the launch traced here: 56.5 us
  Pallas kernels  54.2 us (96%)
  local copies, waits for them, and re-layouts  1.67 us (3%)
  between operations  0.64 us (1%)
    pallas_call x1, Pallas kernels, local(): pl.pallas_call(kernel, out_shape=(pltpu.VMEM((NV, ROWS, columns), F32),)...  54.2 us
    unnamed x2, local copies, waits for them, and re-layouts  1.67 us

profile of v2, /device:TPU:0, one launch (start us, length us, event | category | flops | bytes accessed | tf_op | source)
XLA Modules:
  0.0 56.5 jit_solution(8162040657838402150)
XLA Ops:
  0.6 54.2 %shard_map.113 = (f32[5,16,2048]{2,1,0:T(8,128)S(1)}, f32[5,16,2048]{2,1,0:T(8,128)S(1)}) custom-call(f32[5,16,2048]{2,1,0:T(8,128)} %flow_hbm.1, f32[16,2048]{1,0:T(8,128)} %cspd_hbm.1, f32[16,2048]{1,0:T(8,128)} %aspd_hbm.1, f32[16,2048]{1,0:T(8,128)} %dt_hbm.1, f32[32,64,192]{2,1,0:T(8,128)} %w_hbm.1, s32[1,2048]{1,0:T(1,128)} %bitcast.7, ...), custom_call_target="tpu_custom_call" | custom-call | tf_op jit(solution)/shard_map/pallas_call | solution.py:662
  54.8 0.8 %copy.14 = f32[5,16,2048]{2,1,0:T(8,128)} copy(f32[5,16,2048]{2,1,0:T(8,128)S(1)} %get-tuple-element.2) | data formatting | bytes 1310720
  55.7 0.8 %copy.15 = f32[5,16,2048]{2,1,0:T(8,128)} copy(f32[5,16,2048]{2,1,0:T(8,128)S(1)} %get-tuple-element.3) | data formatting | bytes 1310720

commit v3 on v2

--- a/solution.py
+++ b/solution.py
@@ -19,6 +19,7 @@
 N_AXIAL = 8
 STACK = NV * ROWS
 WIDE = NV * LANES
+BOX = 3 * LANES
 ROW_TILES = 20
 EARLY = 17
 FIRST = 8
@@ -61,8 +62,8 @@
     out_u, out_rate,
     flow, cspd, aspd, dt, w, partner_row, partner_tile, owner, source, host, frac, load_sem,
     cur, base, cs, xs, wts, s32, shi, slo, rc, gout, gend, ends, gloc, fout, floc, a_loc, a_arr, a_edge, c_loc, c_arr,
-    edges, consts, f_keep, halo, perm,
-    ax_send, ax_recv, ini_recv, row_send, row_recv, ci_send, ci_recv, lab_send, lab_recv, outbox, inbox, early_box,
+    edges, consts, f_keep, halo, perm, permuted,
+    ax_send, ax_recv, ini_recv, row_send, row_recv, ci_send, ci_recv, lab_send, lab_recv, outbox, inbox, box_half, early_box,
     ax_ss, ax_rs, ini_ss, ini_rs, row_ss, row_rs, ci_ss, ci_rs, lab_ss, lab_rs, box_ss, box_rs,
 ):
     c = lax.axis_index("circ")
@@ -121,6 +122,7 @@
 
     own = slice(FIRST, FIRST + ROWS)
     lane = lanes_of((ROWS, LANES))
+    box_lane = lanes_of((len(NEIGHBOURS) * CAP, LANES))
 
     loads = [
         pltpu.make_async_copy(src, dst, load_sem.at[i])
@@ -188,7 +190,8 @@
         return ((s & (BLOCKS - 1)) >> 1) * ROWS + (s >> 5)
 
     host_index = row_index(h_row)
-    labels = jnp.sum(chosen * (host_index + 1).astype(F32), axis=1, keepdims=True) - 1.0
+    marks = 2 * (host_index + 1) + (h_row & 1)
+    labels = jnp.sum(chosen * marks.astype(F32), axis=1, keepdims=True)
     lab_send[...] = jnp.broadcast_to(labels, (slots, LANES))
 
     edges[...] = jnp.zeros_like(edges)
@@ -227,8 +230,13 @@
     is_local = t_col == myself
     floc[0] = jnp.where(is_local, straight, 0.0)
     floc[1] = jnp.where(is_local, crossed, 0.0)
-    fout[0] = jnp.dot(chosen, straight, precision=lax.Precision.HIGHEST)
-    fout[1] = jnp.dot(chosen, crossed, precision=lax.Precision.HIGHEST)
+    in_source = (second >> 6) == (s_col & 1)
+    fout[0] = jnp.dot(
+        chosen, jnp.where(in_source, frac_twice, 0.0), precision=lax.Precision.HIGHEST
+    )
+    fout[1] = jnp.dot(
+        chosen, jnp.where(in_source, 0.0, frac_twice), precision=lax.Precision.HIGHEST
+    )
     s_index = row_index(s_col)
     pick = jnp.concatenate(
         [
@@ -314,8 +322,10 @@
     def receive_labels():
         for k in range(len(NEIGHBOURS)):
             label_copy(k).wait()
-        arrived = lab_recv[...]
-        label_row = jnp.concatenate([arrived, arrived], axis=0).T.astype(jnp.int32)
+        arrived = lab_recv[...].astype(jnp.int32)
+        box_half[...] = jnp.where((lanes_of(arrived.shape) >> 6) == (arrived & 1), 1.0, 0.0)
+        places = ((arrived >> 1) - 1).astype(F32)
+        label_row = jnp.concatenate([places, places], axis=0).T.astype(jnp.int32)
         land_here = jnp.where(
             jnp.concatenate([label_row, label_row], axis=0) == tall_rows, 1.0, 0.0
         ).astype(BF16)
@@ -381,17 +391,20 @@
             for p in (0, TILES - 1):
                 pack_rows(n, p, v, cur[p, v, own, :])
 
-    def unpack(n, side):
+    def is_late(p, v):
+        return pair_place(p, v)[0] >= EARLY
+
+    def unpack(n, side, late):
         start = FIRST - 2 if side else FIRST + ROWS
         for p in range(TILES):
             for v in range(NV):
-                where, row = pair_place(p, v)
-                cur[p, v, start:start + 2, :] = ci_recv[n, side, where, row:row + 2, :]
-
-    def permute(n, side):
+                if is_late(p, v) == late:
+                    where, row = pair_place(p, v)
+                    cur[p, v, start:start + 2, :] = ci_recv[n, side, where, row:row + 2, :]
+
+    def permute(n, side, late):
         start = FIRST - 2 if side else FIRST + ROWS
         rows = lax.broadcasted_iota(jnp.int32, (8, LANES), 0)
-        slot_of = [p - 1 if 0 < p < TILES - 1 else TILES - 2 + p // (TILES - 1) for p in range(TILES)]
 
         def one(p):
             tile = jnp.broadcast_to(perm[0, pl.ds(p, 1), :], (8, LANES))
@@ -399,17 +412,24 @@
             slot = jnp.where(
                 tile == 0, TILES - 2, jnp.where(tile == TILES - 1, TILES - 1, tile - 1)
             )
-            total = jnp.zeros((8, LANES), F32)
+            offset = slot - (rows >> 1)
+            if late:
+                total, last = permuted[0, p], permuted[1, p]
+            else:
+                total = last = jnp.zeros((8, LANES), F32)
             for q in range(TILES):
-                where, _ = pair_place(q, 0)
-                found = jnp.take_along_axis(ci_recv[n, side, where], column, axis=1)
-                total = jnp.where(slot == slot_of[q], found, total)
-            last = jnp.zeros((8, LANES), F32)
-            offset = slot - (rows >> 1)
+                if is_late(q, 0) == late:
+                    where, _ = pair_place(q, 0)
+                    found = jnp.take_along_axis(ci_recv[n, side, where], column, axis=1)
+                    total = jnp.where(tile == q, found, total)
             for g in range(4):
-                where = TILES - 2 + g if g < 3 else ROW_TILES - 1
-                found = jnp.take_along_axis(ci_recv[n, side, where], column, axis=1)
-                last = jnp.where(offset == 4 * g, found, last)
+                if (g == 3) == late:
+                    where = TILES - 2 + g if g < 3 else ROW_TILES - 1
+                    found = jnp.take_along_axis(ci_recv[n, side, where], column, axis=1)
+                    last = jnp.where(offset == 4 * g, found, last)
+            if not late:
+                permuted[0, p], permuted[1, p] = total, last
+                return
             last = last + pltpu.roll(last, 4, 0)
             last = last + pltpu.roll(last, 2, 0)
             for v in range(NV - 1):
@@ -422,6 +442,26 @@
             return 0
 
         lax.fori_loop(0, TILES // 4, four, 0)
+
+    def halo_rows(n, late):
+        for side in range(2):
+            circ_copy(n, side, int(late)).wait()
+
+        @pl.when(c > 0)
+        def _():
+            unpack(n, 1, late)
+
+        @pl.when(c < N_CIRC - 1)
+        def _():
+            unpack(n, 0, late)
+
+        @pl.when(c == 0)
+        def _():
+            permute(n, 1, late)
+
+        @pl.when(c == N_CIRC - 1)
+        def _():
+            permute(n, 0, late)
 
     def circ_rates(p, _):
         above = cs[p, own, :]
@@ -474,6 +514,9 @@
         for v in range(NV):
             early_box[:, var_lanes(v)] = gathered(gout, fout, v)
         fix_edges(n, earlier, False)
+        late_rows(n)
+        for side in range(2):
+            circ_copy(n, side, 1).start()
         for v in range(NV):
             shift(0, v, halo[0, v], cur[0, v, own, :])
             shift(TILES, v, cur[end, v, own, :], halo[1, v])
@@ -481,9 +524,13 @@
         slopes(end)
         for v in range(NV):
             picked = jnp.dot(gend[...], ends[:, var_lanes(v)], preferred_element_type=F32)
-            outbox[n, :, var_lanes(v)] = (
-                early_box[:, var_lanes(v)] + picked * fout[0] + rolled(picked, HALF) * fout[1]
-            )
+            sent = early_box[:, var_lanes(v)] + picked * fout[0] + rolled(picked, HALF) * fout[1]
+            columns = slice(v // 2 * LANES, v // 2 * LANES + LANES)
+            if v % 2:
+                outbox[n, :, columns] = jnp.where(box_lane < HALF, previous, sent)
+            elif v == NV - 1:
+                outbox[n, :, columns] = sent
+            previous = sent
         for k in FAR_FIRST:
             box_copy(n, k).start()
 
@@ -491,10 +538,6 @@
         def _():
             for k in FAR_FIRST:
                 label_copy(k).start()
-
-        late_rows(n)
-        for side in range(2):
-            circ_copy(n, side, 1).start()
 
         @pl.when(n == 0)
         def _():
@@ -507,28 +550,25 @@
         for v in range(NV):
             scatter(a_loc, c_loc, v, range(TILES))
 
-        for side in range(2):
-            for late in range(2):
-                circ_copy(n, side, late).wait()
-
-        @pl.when(c > 0)
-        def _():
-            unpack(n, 1)
-
-        @pl.when(c < N_CIRC - 1)
-        def _():
-            unpack(n, 0)
-
-        @pl.when(c == 0)
-        def _():
-            permute(n, 1)
-
-        @pl.when(c == N_CIRC - 1)
-        def _():
-            permute(n, 0)
+        halo_rows(n, False)
+        at_seam = (c == 0) | (c == N_CIRC - 1)
+        whole = [p for p in range(TILES) if not is_late(p, NV - 1)]
+
+        @pl.when(jnp.logical_not(at_seam))
+        def _():
+            for p in whole:
+                circ_rates(p, 0)
+
+        halo_rows(n, True)
+
+        @pl.when(at_seam)
+        def _():
+            for p in whole:
+                circ_rates(p, 0)
 
         for p in range(TILES):
-            circ_rates(p, 0)
+            if p not in whole:
+                circ_rates(p, 0)
 
         for k in range(len(NEIGHBOURS)):
             box_copy(n, k).wait()
@@ -538,7 +578,13 @@
             receive_labels()
 
         for v in range(NV):
-            high, low = split(inbox[n, :, var_lanes(v)])
+            columns = slice(v // 2 * LANES, v // 2 * LANES + LANES)
+            packed = inbox[n, :, columns]
+            if v == NV - 1:
+                both = packed
+            else:
+                both = jnp.where((box_lane < HALF) == (v % 2 == 0), packed, rolled(packed, HALF))
+            high, low = split(both * box_half[...])
             c_arr[:slots, var_lanes(v)] = high
             c_arr[slots:, var_lanes(v)] = low
         for v in range(NV):
@@ -640,6 +686,7 @@
         pltpu.VMEM((2, STACK, LANES), F32),
         pltpu.VMEM((2, NV, ROWS, LANES), F32),
         pltpu.VMEM((2, TILES, LANES), jnp.int32),
+        pltpu.VMEM((2, TILES, 8, LANES), F32),
         pltpu.VMEM((BALANCES + 1, 2, NV, ROWS, LANES), F32),
         pltpu.VMEM((BALANCES + 1, 2, NV, ROWS, LANES), F32),
         pltpu.VMEM((3, ROWS, LANES), F32),
@@ -649,8 +696,9 @@
         pltpu.VMEM((BALANCES, 2, ROW_TILES, 8, LANES), F32),
         pltpu.VMEM((slots, LANES), F32),
         pltpu.VMEM((slots, LANES), F32),
-        pltpu.VMEM((BALANCES, slots, WIDE), F32),
-        pltpu.VMEM((BALANCES, slots, WIDE), F32),
+        pltpu.VMEM((BALANCES, slots, BOX), F32),
+        pltpu.VMEM((BALANCES, slots, BOX), F32),
+        pltpu.VMEM((slots, LANES), F32),
         pltpu.VMEM((slots, WIDE), F32),
         dma((BALANCES + 1, 2)), dma((BALANCES + 1, 2)),
         dma((3,)), dma((3,)),

time: 56.6 us -> 54 us (0.954)
  Pallas kernels: 54.2 us -> 51.6 us
    pallas_call x1, Pallas kernels: 54.2 us -> 51.6 us  [local(): pl.pallas_call(kernel, out_shape=(pltpu.VMEM((NV, ROWS, columns), F32),)...]
where the time goes in v3:
time: 54 us; the launch traced here: 53.9 us
  Pallas kernels  51.6 us (96%)
  local copies, waits for them, and re-layouts  1.67 us (3%)
  between operations  0.64 us (1%)
    pallas_call x1, Pallas kernels, local(): pl.pallas_call(kernel, out_shape=(pltpu.VMEM((NV, ROWS, columns), F32),)...  51.6 us
    unnamed x2, local copies, waits for them, and re-layouts  1.67 us

profile of v3, /device:TPU:0, one launch (start us, length us, event | category | flops | bytes accessed | tf_op | source)
XLA Modules:
  0.0 53.9 jit_solution(6533642788369776143)
XLA Ops:
  0.6 51.6 %shard_map.113 = (f32[5,16,2048]{2,1,0:T(8,128)S(1)}, f32[5,16,2048]{2,1,0:T(8,128)S(1)}) custom-call(f32[5,16,2048]{2,1,0:T(8,128)} %flow_hbm.1, f32[16,2048]{1,0:T(8,128)} %cspd_hbm.1, f32[16,2048]{1,0:T(8,128)} %aspd_hbm.1, f32[16,2048]{1,0:T(8,128)} %dt_hbm.1, f32[32,64,192]{2,1,0:T(8,128)} %w_hbm.1, s32[1,2048]{1,0:T(1,128)} %bitcast.7, ...), custom_call_target="tpu_custom_call" | custom-call | tf_op jit(solution)/shard_map/pallas_call | solution.py:710
  52.2 0.8 %copy.14 = f32[5,16,2048]{2,1,0:T(8,128)} copy(f32[5,16,2048]{2,1,0:T(8,128)S(1)} %get-tuple-element.2) | data formatting | bytes 1310720
  53.1 0.8 %copy.15 = f32[5,16,2048]{2,1,0:T(8,128)} copy(f32[5,16,2048]{2,1,0:T(8,128)S(1)} %get-tuple-element.3) | data formatting | bytes 1310720

commit v4 on v3

--- a/solution.py
+++ b/solution.py
@@ -61,10 +61,12 @@
     host_hbm, frac_hbm,
     out_u, out_rate,
     flow, cspd, aspd, dt, w, partner_row, partner_tile, owner, source, host, frac, load_sem,
-    cur, base, cs, xs, wts, s32, shi, slo, rc, gout, gend, ends, gloc, fout, floc, a_loc, a_arr, a_edge, c_loc, c_arr,
+    cur, base, cs, xs, wts, s32, shi, slo, rc, gout, gend, ends, gloc, fout, floc, a_loc, a_arr, a_edge, a_end, c_loc, c_arr,
     edges, consts, f_keep, halo, perm, permuted,
     ax_send, ax_recv, ini_recv, row_send, row_recv, ci_send, ci_recv, lab_send, lab_recv, outbox, inbox, box_half, early_box,
+    end_send, end_recv, slope_send, slope_recv,
     ax_ss, ax_rs, ini_ss, ini_rs, row_ss, row_rs, ci_ss, ci_rs, lab_ss, lab_rs, box_ss, box_rs,
+    end_ss, end_rs, slope_ss, slope_rs,
 ):
     c = lax.axis_index("circ")
     a = lax.axis_index("axial")
@@ -118,6 +120,22 @@
         rows = pl.ds(k * CAP, CAP)
         return remote(
             outbox.at[n, rows], inbox.at[n, rows], box_ss.at[n, k], box_rs.at[n, k], dc, da
+        )
+
+    def end_target(which, k):
+        dc, da = NEIGHBOURS[k]
+        return dc, da + (1 if which else -1)
+
+    def end_copy(which, k):
+        return remote(
+            end_send.at[which, k], end_recv.at[which, k], end_ss.at[which, k],
+            end_rs.at[which, k], *end_target(which, k),
+        )
+
+    def slope_copy(side):
+        return remote(
+            slope_send.at[side], slope_recv.at[side], slope_ss.at[side], slope_rs.at[side],
+            0, 2 * side - 1,
         )
 
     own = slice(FIRST, FIRST + ROWS)
@@ -319,6 +337,65 @@
             for k in range(8):
                 cs[half * 8 + k, FIRST - 1:FIRST, :] = below_row[k:k + 1]
 
+    def end_matrix():
+        slot_marks = jnp.concatenate([lab_send[...], lab_send[...]], axis=0).T.astype(jnp.int32)
+        slot_marks = jnp.concatenate([slot_marks, slot_marks], axis=0)
+        index = tall_rows & (ROWS - 1)
+        target = jnp.where(
+            tall_rows < SMALL, 2 * (index + 1), 2 * ((TILES - 1) * ROWS + index + 1) + 1
+        )
+        slot_of = (lanes_of(tall) & (slots - 1)) >> 3
+        hit = (slot_marks == target) & (slot_of == ((tall_rows >> 4) & 7))
+        a_end[...] = jnp.where(hit, 1.0, 0.0).astype(BF16)
+
+    def send_ends(n):
+        packed_lane = lanes_of(tall)
+        result = jnp.zeros(tall, F32)
+        for t in range(BOX // LANES):
+            high, low = split(outbox[n, :, t * LANES:(t + 1) * LANES])
+            both = jnp.concatenate([high, low], axis=0)
+            columns = jnp.dot(a_end[...], both, preferred_element_type=F32)
+            for v in range(2 * t, min(2 * t + 2, NV)):
+                moved = rolled(columns, v + HALF) if v % 2 else rolled(columns, v) if v else columns
+                wanted = (packed_lane == v) | (packed_lane == HALF - 1 + v)
+                result = jnp.where(wanted, moved, result)
+        for which in range(2):
+            for k in range(len(NEIGHBOURS)):
+                start = (which * len(NEIGHBOURS) + k) * ROWS
+                end_send[which, k] = result[start:start + ROWS]
+        for k in FAR_FIRST:
+            for which in range(2):
+                if end_target(which, k) != (0, 0):
+                    end_copy(which, k).start()
+
+    def send_slopes():
+        for side in range(2):
+            total = jnp.zeros((ROWS, LANES), F32)
+            for v in range(NV):
+                tile = s32[side * (TILES - 1), var_rows(v), :]
+                moved = rolled(tile, v + side) if v + side else tile
+                total = jnp.where(lane == v, moved, total)
+            slope_send[side] = total
+            slope_copy(side).start()
+
+    def receive_ends():
+        for side in range(2):
+            slope_copy(side).wait()
+        sums = []
+        for which in range(2):
+            total = None
+            for k in range(len(NEIGHBOURS)):
+                if end_target(which, k) == (0, 0):
+                    part = end_send[which, k]
+                else:
+                    end_copy(which, k).wait()
+                    part = end_recv[which, k]
+                total = part if total is None else total + part
+            sums.append(total)
+        slope_right = slope_recv[0] + sums[0]
+        slope_left = slope_recv[1] + rolled(sums[1], LANES - HALF + 1)
+        return slope_left, slope_right
+
     def receive_labels():
         for k in range(len(NEIGHBOURS)):
             label_copy(k).wait()
@@ -334,14 +411,25 @@
         a_edge[2 * ROWS:, :] = land_here[-2 * ROWS:]
 
     def fix_edges(n, factor, also_rate):
-        for side in range(2):
-            axial_copy(n, side).wait()
+        if also_rate:
+            slope_left, slope_right = receive_ends()
+        else:
+            for side in range(2):
+                axial_copy(n, side).wait()
         left_speed, right_speed = consts[2], consts[3]
         last = (TILES - 1) * LANES
         for v in range(NV):
             vr = var_rows(v)
-            from_left = jnp.where(a > 0, ax_recv[n, 1, v], 0.0)
-            from_right = jnp.where(a < N_AXIAL - 1, ax_recv[n, 0, v], 0.0)
+            if also_rate:
+                aligned = rolled(slope_left, LANES - v) if v else slope_left
+                from_left = rolled(halo[0, v], 1) + 0.5 * aligned
+                from_right = rolled(halo[1, v], LANES - 1) - 0.5 * rolled(
+                    slope_right, LANES - 1 - v
+                )
+            else:
+                from_left, from_right = ax_recv[n, 1, v], ax_recv[n, 0, v]
+            from_left = jnp.where(a > 0, from_left, 0.0)
+            from_right = jnp.where(a < N_AXIAL - 1, from_right, 0.0)
             left_flux = jnp.maximum(left_speed, 0.0) * from_left + jnp.minimum(
                 left_speed, 0.0
             ) * edges[0, vr, :]
@@ -542,6 +630,11 @@
         @pl.when(n == 0)
         def _():
             receive_constants()
+            end_matrix()
+
+        @pl.when(n == BALANCES - 1)
+        def _():
+            send_ends(n)
 
         for v in range(NV):
             high, low = split(gathered(gloc, floc, v))
@@ -549,6 +642,10 @@
             c_loc[SMALL:, var_lanes(v)] = low
         for v in range(NV):
             scatter(a_loc, c_loc, v, range(TILES))
+
+        @pl.when(n == BALANCES - 1)
+        def _():
+            send_slopes()
 
         halo_rows(n, False)
         at_seam = (c == 0) | (c == N_CIRC - 1)
@@ -607,8 +704,11 @@
                 lane < HALF, new_first, rolled(right_face, LANES - 1)
             )
             ax_send[n + 1, 1, v] = jnp.where(lane >= HALF, new_last, rolled(left_face, 1))
-        for side in range(2):
-            axial_copy(n + 1, side).start()
+
+        @pl.when(n < BALANCES - 1)
+        def _():
+            for side in range(2):
+                axial_copy(n + 1, side).start()
 
         for v in range(NV):
             scatter(a_arr, c_arr, v, range(2, end - 1))
@@ -679,6 +779,7 @@
         pltpu.VMEM((TILES * ROWS, 2 * SMALL), BF16),
         pltpu.VMEM(((TILES - 4) * ROWS, 2 * slots), BF16),
         pltpu.VMEM((4 * ROWS, 2 * slots), BF16),
+        pltpu.VMEM((TILES * ROWS, 2 * slots), BF16),
         pltpu.VMEM((2 * SMALL, WIDE), BF16),
         pltpu.VMEM((2 * slots, WIDE), BF16),
         pltpu.VMEM((2, STACK, LANES), F32),
@@ -700,12 +801,17 @@
         pltpu.VMEM((BALANCES, slots, BOX), F32),
         pltpu.VMEM((slots, LANES), F32),
         pltpu.VMEM((slots, WIDE), F32),
+        pltpu.VMEM((2, len(NEIGHBOURS), ROWS, LANES), F32),
+        pltpu.VMEM((2, len(NEIGHBOURS), ROWS, LANES), F32),
+        pltpu.VMEM((2, ROWS, LANES), F32),
+        pltpu.VMEM((2, ROWS, LANES), F32),
         dma((BALANCES + 1, 2)), dma((BALANCES + 1, 2)),
         dma((3,)), dma((3,)),
         dma((1,)), dma((1,)),
         dma((BALANCES, 2, 2)), dma((BALANCES, 2, 2)),
         dma((len(NEIGHBOURS),)), dma((len(NEIGHBOURS),)),
         dma((BALANCES, len(NEIGHBOURS))), dma((BALANCES, len(NEIGHBOURS))),
+        dma((2, len(NEIGHBOURS))), dma((2, len(NEIGHBOURS))), dma((2,)), dma((2,)),
     ]
     return pl.pallas_call(
         kernel,

time: 54 us -> 52.6 us (0.974)
  Pallas kernels: 51.6 us -> 50.1 us
    pallas_call x1, Pallas kernels: 51.6 us -> 50.1 us  [local(): pl.pallas_call(kernel, out_shape=(pltpu.VMEM((NV, ROWS, columns), F32),)...]
where the time goes in v4:
time: 52.6 us; the launch traced here: 52.4 us
  Pallas kernels  50.1 us (95%)
  local copies, waits for them, and re-layouts  1.67 us (3%)
  between operations  0.64 us (1%)
    pallas_call x1, Pallas kernels, local(): pl.pallas_call(kernel, out_shape=(pltpu.VMEM((NV, ROWS, columns), F32),)...  50.1 us
    unnamed x2, local copies, waits for them, and re-layouts  1.67 us

profile of v4, /device:TPU:0, one launch (start us, length us, event | category | flops | bytes accessed | tf_op | source)
XLA Modules:
  0.0 52.4 jit_solution(6213260752846297878)
XLA Ops:
  0.6 50.1 %shard_map.113 = (f32[5,16,2048]{2,1,0:T(8,128)S(1)}, f32[5,16,2048]{2,1,0:T(8,128)S(1)}) custom-call(f32[5,16,2048]{2,1,0:T(8,128)} %flow_hbm.1, f32[16,2048]{1,0:T(8,128)} %cspd_hbm.1, f32[16,2048]{1,0:T(8,128)} %aspd_hbm.1, f32[16,2048]{1,0:T(8,128)} %dt_hbm.1, f32[32,64,192]{2,1,0:T(8,128)} %w_hbm.1, s32[1,2048]{1,0:T(1,128)} %bitcast.7, ...), custom_call_target="tpu_custom_call" | custom-call | tf_op jit(solution)/shard_map/pallas_call | solution.py:816
  50.8 0.8 %copy.14 = f32[5,16,2048]{2,1,0:T(8,128)} copy(f32[5,16,2048]{2,1,0:T(8,128)S(1)} %get-tuple-element.2) | data formatting | bytes 1310720
  51.6 0.8 %copy.15 = f32[5,16,2048]{2,1,0:T(8,128)} copy(f32[5,16,2048]{2,1,0:T(8,128)S(1)} %get-tuple-element.3) | data formatting | bytes 1310720

commit v5 on v4

--- a/solution.py
+++ b/solution.py
@@ -59,9 +59,9 @@
 def kernel(
     flow_hbm, cspd_hbm, aspd_hbm, dt_hbm, w_hbm, prow_hbm, ptile_hbm, owner_hbm, source_hbm,
     host_hbm, frac_hbm,
-    out_u, out_rate,
+    out_half, out_circ, out_axial,
     flow, cspd, aspd, dt, w, partner_row, partner_tile, owner, source, host, frac, load_sem,
-    cur, base, cs, xs, wts, s32, shi, slo, rc, gout, gend, ends, gloc, fout, floc, a_loc, a_arr, a_edge, a_end, c_loc, c_arr,
+    cur, base, cs, xs, wts, s32, shi, slo, gout, gend, ends, gloc, fout, floc, a_loc, a_arr, a_edge, a_end, c_loc, c_arr,
     edges, consts, f_keep, halo, perm, permuted,
     ax_send, ax_recv, ini_recv, row_send, row_recv, ci_send, ci_recv, lab_send, lab_recv, outbox, inbox, box_half, early_box,
     end_send, end_recv, slope_send, slope_recv,
@@ -436,14 +436,14 @@
             right_flux = jnp.maximum(right_speed, 0.0) * edges[1, vr, :] + jnp.minimum(
                 right_speed, 0.0
             ) * from_right
-            cur[0, v, own, :] = cur[0, v, own, :] + factor * dt[:, 0:LANES] * left_flux
-            cur[TILES - 1, v, own, :] = (
-                cur[TILES - 1, v, own, :] - factor * dt[:, last:] * right_flux
-            )
             if also_rate:
-                out_rate[v, :, 0:LANES] = out_rate[v, :, 0:LANES] - left_flux
-                out_rate[v, :, last:] = out_rate[v, :, last:] + right_flux
+                out_axial[v, :, 0:LANES] = out_axial[v, :, 0:LANES] - left_flux
+                out_axial[v, :, last:] = out_axial[v, :, last:] + right_flux
             else:
+                cur[0, v, own, :] = cur[0, v, own, :] + factor * dt[:, 0:LANES] * left_flux
+                cur[TILES - 1, v, own, :] = (
+                    cur[TILES - 1, v, own, :] - factor * dt[:, last:] * right_flux
+                )
                 halo[0, v] = from_left - factor * consts[0] * rolled(left_flux, LANES - 1)
                 halo[1, v] = from_right + factor * consts[1] * rolled(right_flux, 1)
 
@@ -563,7 +563,7 @@
             slope_above = 0.25 * (at[4] - at[2])
             upper = above_pos * (at[2] + slope_here) + above_neg * (at[3] - slope_above)
             lower = below_pos * (at[1] + slope_below) + below_neg * (at[2] - slope_here)
-            rc[p, var_rows(v), :] = upper - lower
+            out_circ[v, :, cells(p)] = upper - lower
         return 0
 
     def face(p, v, kind):
@@ -576,22 +576,29 @@
         right = rolled(jnp.where(lane == 0, right_lane, face(p, v, 1)), LANES - 1)
         return jnp.maximum(speed, 0.0) * face(p, v, 0) + jnp.minimum(speed, 0.0) * right
 
+    def axial_rate(flux_here, flux_left):
+        return flux_here - rolled(jnp.where(lane == LANES - 1, flux_left, flux_here), 1)
+
     def advance(p, v, flux_here, flux_left, first_stage, factor):
-        before = rolled(jnp.where(lane == LANES - 1, flux_left, flux_here), 1)
-        rate = rc[p, var_rows(v), :] + flux_here - before
+        rate = out_circ[v, :, cells(p)] + axial_rate(flux_here, flux_left)
         here = cur[p, v, own, :]
         start = jnp.where(first_stage, here, base[p, var_rows(v), :])
         base[p, var_rows(v), :] = start
-        out_rate[v, :, cells(p)] = rate
         new = 0.5 * (start + here) - factor * (dt[:, cells(p)] * rate)
         cur[p, v, own, :] = new
         return new
 
-    def balance(n, _):
-        odd = lax.rem(n, 2)
-        first_stage = odd == 0
-        factor = jnp.where(first_stage, 1.0, 0.5).astype(F32)
-        earlier = jnp.where(first_stage, 0.5, 1.0).astype(F32)
+    def conclude(p, v, flux_here, flux_left):
+        out_axial[v, :, cells(p)] = axial_rate(flux_here, flux_left)
+        out_half[v, :, cells(p)] = 0.5 * (base[p, var_rows(v), :] + cur[p, v, own, :])
+
+    def balance(n, is_last):
+        if is_last:
+            first_stage, factor, earlier = False, 0.5, 1.0
+        else:
+            first_stage = lax.rem(n, 2) == 0
+            factor = jnp.where(first_stage, 1.0, 0.5).astype(F32)
+            earlier = jnp.where(first_stage, 0.5, 1.0).astype(F32)
         end = TILES - 1
 
         for p in range(1, end):
@@ -622,19 +629,21 @@
         for k in FAR_FIRST:
             box_copy(n, k).start()
 
-        @pl.when(n == 0)
-        def _():
-            for k in FAR_FIRST:
-                label_copy(k).start()
-
-        @pl.when(n == 0)
-        def _():
-            receive_constants()
-            end_matrix()
-
-        @pl.when(n == BALANCES - 1)
-        def _():
+        if not is_last:
+
+            @pl.when(n == 0)
+            def _():
+                for k in FAR_FIRST:
+                    label_copy(k).start()
+
+        if is_last:
             send_ends(n)
+        else:
+
+            @pl.when(n == 0)
+            def _():
+                receive_constants()
+                end_matrix()
 
         for v in range(NV):
             high, low = split(gathered(gloc, floc, v))
@@ -643,8 +652,7 @@
         for v in range(NV):
             scatter(a_loc, c_loc, v, range(TILES))
 
-        @pl.when(n == BALANCES - 1)
-        def _():
+        if is_last:
             send_slopes()
 
         halo_rows(n, False)
@@ -670,9 +678,11 @@
         for k in range(len(NEIGHBOURS)):
             box_copy(n, k).wait()
 
-        @pl.when(n == 0)
-        def _():
-            receive_labels()
+        if not is_last:
+
+            @pl.when(n == 0)
+            def _():
+                receive_labels()
 
         for v in range(NV):
             columns = slice(v // 2 * LANES, v // 2 * LANES + LANES)
@@ -698,44 +708,47 @@
             edges[1, vr, :] = left_face
             f_keep[0, vr, :] = flux_first
             f_keep[1, vr, :] = flux_before
+            if is_last:
+                conclude(0, v, flux_first, 0.0)
+                conclude(end, v, flux_last, flux_before)
+                continue
             new_first = advance(0, v, flux_first, 0.0, first_stage, factor)
             new_last = advance(end, v, flux_last, flux_before, first_stage, factor)
             ax_send[n + 1, 0, v] = jnp.where(
                 lane < HALF, new_first, rolled(right_face, LANES - 1)
             )
             ax_send[n + 1, 1, v] = jnp.where(lane >= HALF, new_last, rolled(left_face, 1))
-
-        @pl.when(n < BALANCES - 1)
-        def _():
+        if not is_last:
             for side in range(2):
                 axial_copy(n + 1, side).start()
 
         for v in range(NV):
             scatter(a_arr, c_arr, v, range(2, end - 1))
+
         for v in range(NV):
             before = f_keep[0, var_rows(v), :]
             tile = cur[0, v, own, :]
             for p in range(1, end):
                 here = flux(p, v, face(p + 1, v, 1)) if p < end - 1 else f_keep[1, var_rows(v), :]
+                if is_last:
+                    conclude(p, v, here, before)
+                    before = here
+                    continue
                 new = advance(p, v, here, before, first_stage, factor)
                 pack_rows(n + 1, p, v, new)
                 shift(p, v, tile, new)
                 before, tile = here, new
-            shift(end, v, tile, cur[end, v, own, :])
-
-        @pl.when(n < BALANCES - 1)
-        def _():
+            if not is_last:
+                shift(end, v, tile, cur[end, v, own, :])
+        if not is_last:
             for side in range(2):
                 circ_copy(n + 1, side, 0).start()
 
         return 0
 
-    lax.fori_loop(0, BALANCES, balance, 0)
-    fix_edges(BALANCES, jnp.float32(0.5), True)
-
-    for p in range(TILES):
-        for v in range(NV):
-            out_u[v, :, cells(p)] = cur[p, v, own, :]
+    lax.fori_loop(0, BALANCES - 1, lambda n, _: balance(n, False), 0)
+    balance(BALANCES - 1, True)
+    fix_edges(BALANCES, None, True)
 
 
 def local(
@@ -747,7 +760,6 @@
     vmem = pl.BlockSpec(memory_space=pltpu.VMEM)
     hbm = pl.BlockSpec(memory_space=pltpu.HBM)
     dma = pltpu.SemaphoreType.DMA
-    shape = jax.ShapeDtypeStruct((NV, ROWS, columns), F32)
     scratch = [
         pltpu.VMEM((NV, ROWS, columns), F32),
         pltpu.VMEM((ROWS, columns), F32),
@@ -769,7 +781,6 @@
         pltpu.VMEM((TILES, STACK, LANES), F32),
         pltpu.VMEM((TILES * ROWS, WIDE), BF16),
         pltpu.VMEM((TILES * ROWS, WIDE), BF16),
-        pltpu.VMEM((TILES, STACK, LANES), F32),
         pltpu.VMEM((slots, TILES * ROWS), BF16),
         pltpu.VMEM((slots, 4 * ROWS), BF16),
         pltpu.VMEM((4 * ROWS, WIDE), BF16),
@@ -813,11 +824,11 @@
         dma((BALANCES, len(NEIGHBOURS))), dma((BALANCES, len(NEIGHBOURS))),
         dma((2, len(NEIGHBOURS))), dma((2, len(NEIGHBOURS))), dma((2,)), dma((2,)),
     ]
-    return pl.pallas_call(
+    half, circ_rate, axial_rate = pl.pallas_call(
         kernel,
-        out_shape=(pltpu.VMEM((NV, ROWS, columns), F32),) * 2,
+        out_shape=(pltpu.VMEM((NV, ROWS, columns), F32),) * 3,
         in_specs=[hbm] * 11,
-        out_specs=(vmem, vmem),
+        out_specs=(vmem, vmem, vmem),
         scratch_shapes=scratch,
         compiler_params=pltpu.CompilerParams(
             collective_id=0, has_side_effects=True, vmem_limit_bytes=56 * 1024 * 1024
@@ -828,6 +839,8 @@
         merge_owner.reshape(1, SMALL), merge_source.reshape(1, SMALL),
         merge_host.reshape(1, SMALL), merge_frac.T,
     )
+    last_rate = circ_rate + axial_rate
+    return half - 0.5 * (time_step * last_rate), last_rate
 
 
 def solution(mesh):

time: 52.6 us -> 51.5 us (0.979)
  local copies, waits for them, and re-layouts: 1.67 us -> 0.01 us
  other arithmetic: 0 us -> 1.22 us
  Pallas kernels: 50.1 us -> 49.5 us
    unnamed x2, local copies, waits for them, and re-layouts: 1.67 us -> 0.01 us
    sub x0 -> x1, other arithmetic: none -> 1.22 us  [local(): return (half - 0.5 * (time_step * last_rate), last_rate)]
    pallas_call x1, Pallas kernels: 50.1 us -> 49.5 us  [local(): pl.pallas_call(kernel, out_shape=(pltpu.VMEM((NV, ROWS, columns), F32),)...]
where the time goes in v5:
time: 51.5 us; the launch traced here: 51.4 us
  Pallas kernels  49.5 us (96%)
  other arithmetic  1.22 us (2%)
  between operations  0.66 us (1%)
    pallas_call x1, Pallas kernels, local(): pl.pallas_call(kernel, out_shape=(pltpu.VMEM((NV, ROWS, columns), F32),)...  49.5 us
    sub x1, other arithmetic, local(): return (half - 0.5 * (time_step * last_rate), last_rate)  1.22 us

profile of v5, /device:TPU:0, one launch (start us, length us, event | category | flops | bytes accessed | tf_op | source)
XLA Modules:
  0.0 51.4 jit_solution(3545777725640067659)
XLA Ops:
  0.6 0.0 copy-start
  0.6 49.5 %shard_map.113 = (f32[5,16,2048]{2,1,0:T(8,128)S(1)}, f32[5,16,2048]{2,1,0:T(8,128)S(1)}, f32[5,16,2048]{2,1,0:T(8,128)S(1)}) custom-call(f32[5,16,2048]{2,1,0:T(8,128)} %flow_hbm.1, f32[16,2048]{1,0:T(8,128)} %cspd_hbm.1, f32[16,2048]{1,0:T(8,128)} %aspd_hbm.1, f32[16,2048]{1,0:T(8,128)} %dt_hbm.1, f32[32,64,192]{2,1,0:T(8,128)} %w_hbm.1, ...), custom_call_target="tpu_custom_call" | custom-call | tf_op jit(solution)/shard_map/pallas_call | solution.py:827
  50.1 0.0 copy-done
  50.2 1.2 %multiply_subtract_fusion = (f32[5,16,2048]{2,1,0:T(8,128)}, f32[5,16,2048]{2,1,0:T(8,128)}) fusion(f32[5,16,2048]{2,1,0:T(8,128)S(1)} %get-tuple-element.5, f32[16,2048]{1,0:T(8,128)S(1)} %copy-done, f32[5,16,2048]{2,1,0:T(8,128)S(1)} %get-tuple-element.6, f32[5,16,2048]{2,1,0:T(8,128)S(1)} %get-tuple-element.7), kind=kLoop, calls=%fused_computation | loop fusion | flops 655360 | bytes 3407872 | tf_op jit(solution)/shard_map/sub | solution.py:843
Async XLA Ops:
  0.6 49.5 %copy-start = (f32[16,2048]{1,0:T(8,128)S(1)}, f32[16,2048]{1,0:T(8,128)}, u32[]{:S(2)}) copy-start(f32[16,2048]{1,0:T(8,128)} %dt_hbm.1) | copy-start | bytes 393220

commit v6 on v5

--- a/solution.py
+++ b/solution.py
@@ -551,20 +551,20 @@
         def _():
             permute(n, 0, late)
 
-    def circ_rates(p, _):
-        above = cs[p, own, :]
-        below = cs[p, FIRST - 1:FIRST + ROWS - 1, :]
+    def circ_rates(p, start=0, count=ROWS):
+        at_row = FIRST + start
+        above = cs[p, at_row:at_row + count, :]
+        below = cs[p, at_row - 1:at_row - 1 + count, :]
         above_pos, above_neg = jnp.maximum(above, 0.0), jnp.minimum(above, 0.0)
         below_pos, below_neg = jnp.maximum(below, 0.0), jnp.minimum(below, 0.0)
         for v in range(NV):
-            at = [cur[p, v, FIRST + k:FIRST + k + ROWS, :] for k in (-2, -1, 0, 1, 2)]
+            at = [cur[p, v, at_row + k:at_row + k + count, :] for k in (-2, -1, 0, 1, 2)]
             slope_below = 0.25 * (at[2] - at[0])
             slope_here = 0.25 * (at[3] - at[1])
             slope_above = 0.25 * (at[4] - at[2])
             upper = above_pos * (at[2] + slope_here) + above_neg * (at[3] - slope_above)
             lower = below_pos * (at[1] + slope_below) + below_neg * (at[2] - slope_here)
-            out_circ[v, :, cells(p)] = upper - lower
-        return 0
+            out_circ[v, start:start + count, cells(p)] = upper - lower
 
     def face(p, v, kind):
         half_slope = 0.5 * s32[p, var_rows(v), :]
@@ -656,26 +656,25 @@
             send_slopes()
 
         halo_rows(n, False)
-        at_seam = (c == 0) | (c == N_CIRC - 1)
         whole = [p for p in range(TILES) if not is_late(p, NV - 1)]
-
-        @pl.when(jnp.logical_not(at_seam))
+        for p in whole:
+            circ_rates(p)
+        halo_rows(n, True)
+        for p in range(TILES):
+            if p not in whole:
+                circ_rates(p)
+
+        @pl.when(c == 0)
         def _():
             for p in whole:
-                circ_rates(p, 0)
-
-        halo_rows(n, True)
-
-        @pl.when(at_seam)
+                circ_rates(p, 0, 8)
+
+        @pl.when(c == N_CIRC - 1)
         def _():
             for p in whole:
-                circ_rates(p, 0)
-
-        for p in range(TILES):
-            if p not in whole:
-                circ_rates(p, 0)
-
-        for k in range(len(NEIGHBOURS)):
+                circ_rates(p, 8, 8)
+
+        for k in reversed(FAR_FIRST):
             box_copy(n, k).wait()
 
         if not is_last:

time: 51.5 us -> 51.4 us (level)
  no operation moved by 1% of the time
where the time goes in v6:
time: 51.4 us; the launch traced here: 51.3 us
  Pallas kernels  49.5 us (96%)
  other arithmetic  1.22 us (2%)
  between operations  0.66 us (1%)
    pallas_call x1, Pallas kernels, local(): pl.pallas_call(kernel, out_shape=(pltpu.VMEM((NV, ROWS, columns), F32),)...  49.5 us
    sub x1, other arithmetic, local(): return (half - 0.5 * (time_step * last_rate), last_rate)  1.22 us

profile of v6, /device:TPU:0, one launch (start us, length us, event | category | flops | bytes accessed | tf_op | source)
XLA Modules:
  0.0 51.3 jit_solution(17326657669065008219)
XLA Ops:
  0.6 0.0 copy-start
  0.6 49.5 %shard_map.113 = (f32[5,16,2048]{2,1,0:T(8,128)S(1)}, f32[5,16,2048]{2,1,0:T(8,128)S(1)}, f32[5,16,2048]{2,1,0:T(8,128)S(1)}) custom-call(f32[5,16,2048]{2,1,0:T(8,128)} %flow_hbm.1, f32[16,2048]{1,0:T(8,128)} %cspd_hbm.1, f32[16,2048]{1,0:T(8,128)} %aspd_hbm.1, f32[16,2048]{1,0:T(8,128)} %dt_hbm.1, f32[32,64,192]{2,1,0:T(8,128)} %w_hbm.1, ...), custom_call_target="tpu_custom_call" | custom-call | tf_op jit(solution)/shard_map/pallas_call | solution.py:826
  50.1 0.0 copy-done
  50.1 1.2 %multiply_subtract_fusion = (f32[5,16,2048]{2,1,0:T(8,128)}, f32[5,16,2048]{2,1,0:T(8,128)}) fusion(f32[5,16,2048]{2,1,0:T(8,128)S(1)} %get-tuple-element.5, f32[16,2048]{1,0:T(8,128)S(1)} %copy-done, f32[5,16,2048]{2,1,0:T(8,128)S(1)} %get-tuple-element.6, f32[5,16,2048]{2,1,0:T(8,128)S(1)} %get-tuple-element.7), kind=kLoop, calls=%fused_computation | loop fusion | flops 655360 | bytes 3407872 | tf_op jit(solution)/shard_map/sub | solution.py:842
Async XLA Ops:
  0.6 49.5 %copy-start = (f32[16,2048]{1,0:T(8,128)S(1)}, f32[16,2048]{1,0:T(8,128)}, u32[]{:S(2)}) copy-start(f32[16,2048]{1,0:T(8,128)} %dt_hbm.1) | copy-start | bytes 393220
